TPU v7x, 256 devices: a whole 4x4x8 slice. The times are simulated.
256 devices in a mesh: dp: 16 (over y, z_lo), tensor: 16 (over z_hi, x, core).
Axes of the slice: x: 4, y: 4, z: 8 (z_hi: 2, z_lo: 4; z = z_hi * 4 + z_lo), core: 2. Of those that a mesh axis runs over, the one named last changes fastest.
Arguments:
- context: bfloat16 [8192, 6144], P('dp', 'tensor'), may hold values from -6 to 6
- w_out: bfloat16 [6144, 6144], P('tensor'), may hold values from -0.078125 to 0.078125
- encoder: bfloat16 [2048, 384], replicated, may hold values from -0.3125 to 0.3125
- decoder: bfloat16 [2048, 384], replicated, may hold values from -0.5 to 0.5
- cotangent: bfloat16 [8192, 6144], P(('dp', 'tensor')), may hold values from -6 to 6
Outputs:
- layer_out: bfloat16 [8192, 6144], P(('dp', 'tensor'))
- context_grad: bfloat16 [8192, 6144], P('dp', 'tensor')
- w_out_grad: float32 [6144, 6144], P('tensor', 'dp')
- encoder_grad: float32 [2048, 384], P(('dp', 'tensor'))
- decoder_grad: float32 [2048, 384], P(('dp', 'tensor'))
All inputs are finite; a program needn't handle non-finite values.
Results may differ from a plain program's by a relative error of at most 0.02.
Values may be sent and summed in bfloat16 or wider, within the bound.
No kernel may reach another device: no remote copies, remote signals or barrier semaphores. Data moves between devices by JAX's collectives and lax.ppermute only.
A program may use at most 128 MiB of HBM per device.

v0:
```python
import jax
import jax.numpy as jnp
from jax import lax
from jax.sharding import PartitionSpec as P

GROUPS = 16


def on_device(context, w_out, encoder, decoder, cotangent):
    seq_rows = context.shape[0]
    model_width = w_out.shape[1]
    code_width = encoder.shape[0]
    group_feat = encoder.shape[1]
    group_code = code_width // GROUPS
    tensor_count = lax.axis_size("tensor")
    enc_blocks = encoder.reshape(GROUPS, group_code, group_feat)
    dec_blocks = decoder.reshape(GROUPS, group_code, group_feat)
    partial_value = jnp.dot(context, w_out, preferred_element_type=jnp.float32).astype(jnp.bfloat16)
    selected = partial_value.reshape(
        seq_rows // tensor_count * lax.axis_size("tensor"), GROUPS, group_feat
    )
    coded = jnp.einsum("tgd,gcd->tgc", selected, enc_blocks, preferred_element_type=jnp.float32)
    code_rows = lax.psum_scatter(
        coded.reshape(seq_rows // tensor_count * lax.axis_size("tensor"), code_width).astype(
            jnp.bfloat16
        ),
        "tensor",
        scatter_dimension=0,
        tiled=True,
    )
    local_rows = code_rows.shape[0]
    code_blocks = code_rows.reshape(local_rows, GROUPS, group_code)
    layer_out = (
        jnp.einsum("tgc,gcd->tgd", code_blocks, dec_blocks, preferred_element_type=jnp.float32)
        .reshape(local_rows, model_width)
        .astype(jnp.bfloat16)
    )
    cot_blocks = cotangent.reshape(local_rows, GROUPS, group_feat)
    grad_codes = jnp.einsum(
        "tgd,gcd->tgc", cot_blocks, dec_blocks, preferred_element_type=jnp.float32
    ).astype(jnp.bfloat16)
    decoder_term = jnp.einsum(
        "tgc,tgd->gcd", code_blocks, cot_blocks, preferred_element_type=jnp.float32
    ).reshape(code_width, group_feat)
    piece = lax.all_gather(grad_codes.reshape(local_rows, code_width), "tensor", axis=0, tiled=True)
    count = piece.shape[0]
    piece_blocks = piece.reshape(count, GROUPS, group_code)
    back = jnp.einsum("tgc,gcd->tgd", piece_blocks, enc_blocks, preferred_element_type=jnp.float32)
    back = back.reshape(count, model_width).astype(jnp.bfloat16)
    selected = partial_value.reshape(count, GROUPS, group_feat)
    term = jnp.einsum("tgc,tgd->gcd", piece_blocks, selected, preferred_element_type=jnp.float32)
    encoder_term = term
    encoder_term = encoder_term.reshape(code_width, group_feat)
    decoder_grad, encoder_grad = (
        lax.psum_scatter(decoder_term, ("dp", "tensor"), scatter_dimension=0, tiled=True),
        lax.psum_scatter(encoder_term, ("dp", "tensor"), scatter_dimension=0, tiled=True),
    )
    context_grad = lax.dot_general(
        back, w_out, (((1,), (1,)), ((), ())), preferred_element_type=jnp.float32
    ).astype(jnp.bfloat16)
    weight_term = lax.dot_general(
        context, back, (((0,), (0,)), ((), ())), preferred_element_type=jnp.float32
    )
    w_out_grad = lax.psum_scatter(
        weight_term.astype(jnp.bfloat16), "dp", scatter_dimension=1, tiled=True
    ).astype(jnp.float32)
    return (layer_out, context_grad, w_out_grad, encoder_grad, decoder_grad)


def solution(mesh):
    placed = (P("dp", "tensor"), P("tensor", None), P(), P(), P(("dp", "tensor"), None))
    return jax.shard_map(
        on_device,
        mesh=mesh,
        in_specs=placed,
        out_specs=(
            P(("dp", "tensor"), None),
            P("dp", "tensor"),
            P("tensor", "dp"),
            P(("dp", "tensor"), None),
            P(("dp", "tensor"), None),
        ),
        check_vma=False,
    )
```

profile of v0, /device:TPU:30, one launch (start us, length us, event | category | flops | bytes accessed | tf_op | source)
XLA Modules:
  0.0 574.4 jit_solution(11104129489817638244)
XLA Ops:
  7.2 0.0 copy-start
  7.2 0.0 reduce-scatter.3.cloned.1.call-start
  7.2 6.0 %convolution_convert_fusion = bf16[512,6144]{1,0:T(8,128)(2,1)S(1)} fusion(bf16[512,384]{1,0:T(8,128)(2,1)} %param.5, bf16[384,6144]{1,0:T(8,128)(2,1)} %param.6), kind=kOutput, calls=%fused_computation | convolution fusion | flops 2419064832 | bytes 11403264 | tf_op jit(solution)/shard_map/dot_general | solution.py:18
  13.2 0.0 copy-done
  13.2 0.0 copy-start.3
  13.3 3.5 fusion.7
  16.7 0.0 copy-done.3
  16.7 0.0 copy-start.2
  16.7 0.0 copy-start.4
  16.7 4.1 copy.31
  20.8 0.0 reduce-scatter.3.cloned.1.call-update
  20.9 0.0 all-gather.2.cloned.1.call-start
  20.9 0.0 copy-done.2
  20.9 0.0 copy-done.4
  20.9 0.6 fusion.11
  21.6 0.7 copy.77
  22.3 0.0 all-gather.2.cloned.1.call-update
  22.3 0.0 all-reduce.5.cloned.1.call-start
  22.4 88.4 %reduce-scatter.3.cloned.1.call-done = bf16[32,2048]{1,0:T(8,128)(2,1)} async-done(((bf16[512,2048]{1,0:T(8,128)(2,1)}), bf16[32,2048]{1,0:T(8,128)(2,1)}) %reduce-scatter.3.cloned.1.call-update) | async-done | bytes 131088 | tf_op jit(solution)/shard_map/reduce_scatter | solution.py:23
  110.8 3.3 fusion.12
  114.0 59.1 %all-gather.2.cloned.1.call-done = bf16[512,2048]{1,0:T(8,128)(2,1)} async-done(((bf16[32,2048]{1,0:T(8,128)(2,1)}), bf16[512,2048]{1,0:T(8,128)(2,1)}) %all-gather.2.cloned.1.call-update) | async-done | bytes 2097168 | tf_op jit(solution)/shard_map/all_gather | solution.py:45
  173.1 4.0 copy.36
  177.0 6.3 %fusion.1 = f32[16,128,384]{2,1,0:T(8,128)} fusion(bf16[512,16,128]{0,2,1:T(8,128)(2,1)} %bitcast.63, bf16[64,16,8,384]{3,2,1,0:T(8,128)(2,1)} %bitcast.72), kind=kOutput, calls=%fused_computation.3 | convolution fusion | flops 805306368 | bytes 11534336 | tf_op jit(solution)/shard_map/tgc,tgd->gcd/dot_general | solution.py:51
  183.3 0.0 all-reduce.5.cloned.1.call-update
  183.3 0.0 copy-start.6
  183.3 0.2 reduce-scatter.5.cloned.1.call-start
  183.6 3.4 convolution_convert_fusion.2
  187.0 0.0 copy-start.1
  187.0 2.6 copy-done.1
  189.6 0.0 copy-done.6
  189.7 5.2 fusion
  194.8 0.0 copy-start.5
  194.8 0.0 reduce-scatter.5.cloned.1.call-update
  194.9 0.9 copy-done.5
  195.7 0.4 fusion.10
  196.1 0.8 copy.48
  196.9 8.5 %convolution_convert_fusion.4 = bf16[512,384]{1,0:T(8,128)(2,1)} fusion(bf16[512,6144]{0,1:T(8,128)(2,1)} %bitcast.68, bf16[384,6144]{1,0:T(8,128)(2,1)} %param.6), kind=kOutput, calls=%fused_computation.12 | convolution fusion | flops 2416115712 | bytes 11403264 | tf_op jit(solution)/shard_map/dot_general | solution.py:58
  205.4 247.5 %all-reduce.5.cloned.1.call-done = (f32[2048,384]{1,0:T(8,128)}, f32[2048,384]{1,0:T(8,128)}) async-done(((f32[2048,384]{1,0:T(8,128)}, f32[2048,384]{1,0:T(8,128)}), (f32[2048,384]{1,0:T(8,128)}, f32[2048,384]{1,0:T(8,128)})) %all-reduce.5.cloned.1.call-update) | async-done | bytes 6291472
  452.9 1.3 constant_dynamic-slice_fusion
  454.2 111.8 %reduce-scatter.5.cloned.1.call-done = bf16[384,384]{0,1:T(8,128)(2,1)} async-done(((bf16[384,6144]{0,1:T(8,128)(2,1)}), bf16[384,384]{0,1:T(8,128)(2,1)}) %reduce-scatter.5.cloned.1.call-update) | async-done | bytes 294928 | tf_op jit(solution)/shard_map/reduce_scatter | solution.py:64
  566.0 1.9 copy.42
Async XLA Ops:
  7.2 6.1 %copy-start = (bf16[2048,384]{1,0:T(8,128)(2,1)S(1)}, bf16[2048,384]{1,0:T(8,128)(2,1)}, u32[]{:S(2)}) copy-start(bf16[2048,384]{1,0:T(8,128)(2,1)} %param.7) | copy-start | bytes 4718596
  7.2 103.6 %reduce-scatter.3.cloned.1.call-start = ((), (), s32[]{:S(2)}) async-start(), calls=%async_computation.2 | async-start | bytes 2228224 | tf_op jit(solution)/shard_map/reduce_scatter | solution.py:23
  13.2 3.5 copy-start.3
  16.7 4.2 copy-start.2
  16.7 4.2 copy-start.4
  20.9 152.2 %all-gather.2.cloned.1.call-start = ((), (), s32[]{:S(2)}) async-start(), calls=%async_computation.3 | async-start | bytes 2228224 | tf_op jit(solution)/shard_map/all_gather | solution.py:45
  22.3 430.6 %all-reduce.5.cloned.1.call-start = ((), (), s32[]{:S(2)}) async-start(), calls=%async_computation.5 | async-start | bytes 12582912
  183.3 6.3 %copy-start.6 = (bf16[512,384]{1,0:T(8,128)(2,1)S(1)}, bf16[512,384]{1,0:T(8,128)(2,1)}, u32[]{:S(2)}) copy-start(bf16[512,384]{1,0:T(8,128)(2,1)} %param.5) | copy-start | bytes 1179652
  183.3 382.6 %reduce-scatter.5.cloned.1.call-start = ((), (), s32[]{:S(2)}) async-start(), calls=%async_computation.4 | async-start | bytes 5013504 | tf_op jit(solution)/shard_map/reduce_scatter | solution.py:64
  187.0 2.6 copy-start.1
  194.8 0.9 copy-start.5
Sparse Core Ops, SparseCore 0:
  21.0 89.7 reduce-scatter.2
  114.1 58.9 all-gather.1
  183.4 269.3 all-reduce.4
  455.5 110.4 reduce-scatter.4
where the time goes:
time: 578 us; the launch traced here: 574 us
  waiting for transfers between devices  507 us (88%)
  matrix products  37.1 us (6%)
  local copies, waits for them, and re-layouts  16.4 us (3%)
  between operations  13.9 us (2%)
    unnamed x5, waiting for transfers between devices  248 us
    reduce_scatter x1, waiting for transfers between devices, on_device(): lax.psum_scatter(weight_term.astype(jnp.bfloat16), 'dp', scatter_dimensio...  112 us
    reduce_scatter x1, waiting for transfers between devices, on_device(): lax.psum_scatter(coded.reshape(seq_rows // tensor_count * lax.axis_size('...  88.4 us
    all_gather x1, waiting for transfers between devices, on_device(): lax.all_gather(grad_codes.reshape(local_rows, code_width), 'tensor', axis...  59.1 us
  transfers between devices with their start and end apart: 4, of which 4 were waited for; matrix products, arithmetic and copies ran while one was open for 4% of the time, Pallas kernels for 0%

commit v1 on v0

v1 whole, which is shorter than its diff:
```python
import jax
import jax.numpy as jnp
from jax import lax
from jax.experimental import pallas as pl
from jax.experimental.pallas import tpu as pltpu
from jax.sharding import PartitionSpec as P

GROUPS = 16
BF = jnp.bfloat16
F32 = jnp.float32
MIB = 1024 * 1024
FIRST_VMEM = 125 * MIB // 2

TENSOR_RELS = [(dz, dx, dc) for dz in range(2) for dx in range(4) for dc in range(2)]


def tensor_add(t, rel, sign=1):
    dz, dx, dc = rel
    zh, x, c = t // 8, (t // 2) % 4, t % 2
    return ((zh + 2 + sign * dz) % 2) * 8 + ((x + 4 + sign * dx) % 4) * 2 + (c + 2 + sign * dc) % 2


def dp_add(i, rel, sign=1):
    dy, dz = rel
    y, zl = i // 4, i % 4
    return ((y + 4 + sign * dy) % 4) * 4 + (zl + 4 + sign * dz) % 4


def send_tensor(v, rel):
    return lax.ppermute(v, "tensor", [(s, tensor_add(s, rel)) for s in range(16)])


def fetch_tensor(v, rel):
    return lax.ppermute(v, "tensor", [(s, tensor_add(s, rel, -1)) for s in range(16)])


def swap_x(v, r):
    return lax.ppermute(v, "tensor", [(s, s ^ (2 * r)) for s in range(16)])


def swap_y(v, r):
    return lax.ppermute(v, "dp", [(s, s ^ (4 * r)) for s in range(16)])


def send_dp(v, rel):
    return lax.ppermute(v, "dp", [(s, dp_add(s, rel)) for s in range(16)])


def tadd(t, rel):
    dz, dx, dc = rel
    zh, x, c = t // 8, lax.rem(t // 2, 4), lax.rem(t, 2)
    return lax.rem(zh + dz, 2) * 8 + lax.rem(x + dx, 4) * 2 + lax.rem(c + dc, 2)


def dadd(i, rel):
    dy, dz = rel
    y, zl = i // 4, lax.rem(i, 4)
    return lax.rem(y + dy, 4) * 4 + lax.rem(zl + dz, 4)


def ds(start, size):
    return pl.ds(pl.multiple_of(start * size, size), size)


def dot(a, b, dims):
    return lax.dot_general(a, b, (dims, ((), ())), preferred_element_type=F32)


def params(mib):
    return pltpu.CompilerParams(vmem_limit_bytes=mib * MIB)


def cost(flops, nbytes):
    return pl.CostEstimate(flops=flops, bytes_accessed=nbytes, transcendentals=0)


def vmem(n):
    return [pl.BlockSpec(memory_space=pltpu.VMEM)] * n


def shape(*dims, dtype=BF):
    return jax.ShapeDtypeStruct(dims, dtype)


def grad_code_kernel(cot_hbm, dec_hbm, out, *rest):
    chunks, (cot, dec, sems) = rest[:4], rest[4:]
    copies = [pltpu.make_async_copy(cot_hbm, cot, sems.at[4])] + [
        pltpu.make_async_copy(
            dec_hbm.at[k * 512:(k + 1) * 512, :], dec.at[k * 512:(k + 1) * 512, :], sems.at[k]
        )
        for k in range(4)
    ]
    for copy in copies:
        copy.start()
    copies[0].wait()
    by_group(cot, 384, chunks)
    for g in range(GROUPS):
        if g % 4 == 0:
            copies[1 + g // 4].wait()
        out[:, g * 128:(g + 1) * 128] = dot(
            cot[:, g * 384:(g + 1) * 384], dec[g * 128:(g + 1) * 128, :], ((1,), (1,))
        ).astype(BF)


def any_space(n):
    return [pl.BlockSpec(memory_space=pl.ANY)] * n


def by_group(source, width, outs):
    i = lax.axis_index("dp")
    for dy in range(4):
        for dz in range(4):
            outs[dy][:, dz * width:(dz + 1) * width] = source[:, ds(dadd(i, (dy, dz)), width)]


def regroup(blocks, outs):
    n = outs[0].shape[1]
    for k in range(4):
        for b in range(4):
            outs[k][b * 32:(b + 1) * 32, :] = blocks[b][:, k * n:(k + 1) * n]


def code_regroup_kernel(*refs):
    regroup(refs[:4], refs[4:])


def code_regroup(blocks):
    return pl.pallas_call(
        code_regroup_kernel,
        in_specs=vmem(4),
        out_specs=vmem(4),
        out_shape=[shape(128, 128)] * 4,
        compiler_params=params(4),
        cost_estimate=cost(0, MIB // 4),
        name="code_regroup",
    )(*blocks)


def over_y(chunks):
    return [chunks[0]] + [send_dp(chunks[k], (k, 0)) for k in (1, 2, 3)]


def over_z(chunks):
    return [chunks[0]] + [send_dp(chunks[k], (0, k)) for k in (1, 2, 3)]


def wenc_kernel(w_hbm, ctx, enc, after, wenc, ctx_t, ctx_r, w, sems):
    copies = [
        pltpu.make_async_copy(
            w_hbm.at[:, k * 1536:(k + 1) * 1536], w.at[:, k * 1536:(k + 1) * 1536], sems.at[k]
        )
        for k in range(4)
    ]
    for copy in copies:
        copy.start()
    t = lax.axis_index("tensor")
    zh, x, c = t // 8, lax.rem(t // 2, 4), lax.rem(t, 2)
    n = 0
    for dc in range(2):
        for dz, order in ((1, (1, 2, 0, 3)), (0, (3, 2, 0, 1))):
            for r in order:
                chunk = lax.rem(zh + dz, 2) * 8 + (x ^ r) * 2 + lax.rem(c + dc, 2)
                ctx_r[n * 32:(n + 1) * 32, :] = ctx[ds(chunk, 32), :]
                n += 1
    ctx_t[...] = ctx[...].T
    for g in range(GROUPS):
        if g % 4 == 0:
            copies[g // 4].wait()
        wenc[:, g * 128:(g + 1) * 128] = dot(
            w[:, g * 384:(g + 1) * 384], enc[g * 128:(g + 1) * 128, :], ((1,), (1,))
        ).astype(BF)


def wenc_of(w, ctx, enc, after):
    return pl.pallas_call(
        wenc_kernel,
        in_specs=[pl.BlockSpec(memory_space=pltpu.HBM)] + vmem(2) + any_space(1),
        out_specs=vmem(3),
        out_shape=[shape(384, 2048), shape(384, 512), shape(512, 384)],
        scratch_shapes=[pltpu.VMEM((384, 6144), BF), pltpu.SemaphoreType.DMA((4,))],
        compiler_params=params(16),
        cost_estimate=cost(604_000_000, 9 * MIB),
        name="wenc",
    )(w, ctx, enc, after)


def coded_kernel(*refs):
    ctx_r, wenc, mine, theirs, blocks = refs[0], refs[1], refs[2], refs[3], refs[4:8]
    own, other, pair, chunks = refs[8], refs[9], refs[10], refs[11:]
    pair[:32, :] = mine[...]
    pair[32:, :] = theirs[...]
    regroup(blocks, chunks)
    for k in range(4):
        cols = slice(k * 512, (k + 1) * 512)
        coded = dot(ctx_r[...], wenc[:, cols], ((1,), (0,))).astype(BF)
        own[:, cols] = coded[:256]
        other[:, cols] = coded[256:]


def coded_of(ctx_r, wenc, mine, theirs, blocks):
    return pl.pallas_call(
        coded_kernel,
        in_specs=vmem(8),
        out_specs=vmem(7),
        out_shape=[shape(256, 2048)] * 2 + [shape(64, 2048)] + [shape(128, 384)] * 4,
        compiler_params=params(16),
        cost_estimate=cost(805_000_000, 4 * MIB),
        name="coded",
    )(ctx_r, wenc, mine, theirs, *blocks)


def pack_kernel(*refs):
    pieces, own, got, packed, outs = refs[:4], refs[4], refs[5], refs[-5], refs[-4:]
    for k in range(4):
        packed[k * 64:(k + 1) * 64, :] = pieces[k][...]
    for k in range(4):
        rows = slice(k * 64, (k + 1) * 64)
        outs[k][...] = (own[rows, :].astype(F32) + got[rows, :].astype(F32)).astype(BF)


def pack(pieces, own, got, *after):
    return pl.pallas_call(
        pack_kernel,
        in_specs=vmem(6) + any_space(len(after)),
        out_specs=vmem(5),
        out_shape=[shape(256, 2048)] + [shape(64, 2048)] * 4,
        compiler_params=params(12),
        cost_estimate=cost(0, 2 * MIB),
        name="pack",
    )(*pieces, own, got, *after)


def gather_rows(near, far, whole):
    t = lax.axis_index("tensor")
    for dc, half in enumerate((near, far)):
        for dx in range(4):
            for dz in range(2):
                n = dx * 64 + dz * 32
                whole[ds(tadd(t, (dz, dx, dc)), 32), :] = half[n:n + 32, :]


def moment_kernel(near, far, ctx_t, a_send, a_keep, b_send, b_keep, whole):
    gather_rows(near, far, whole)
    i = lax.axis_index("dp")
    y, zl = i // 4, lax.rem(i, 4)
    places = {
        1: ((a_send, 0), (b_keep, 1)),
        2: ((a_send, 1), (b_send, 1)),
        3: ((a_keep, 1), (b_send, 0)),
        0: ((a_keep, 0), (b_keep, 0)),
    }
    for r, halves in places.items():
        cols = jnp.concatenate(
            [whole[:, ds((y ^ r) * 4 + lax.rem(zl + dz, 4), 128)] for dz in range(4)], axis=1
        )
        out = dot(ctx_t[...], cols, ((1,), (0,))).astype(BF)
        for h, (ref, n) in enumerate(halves):
            ref[n * 384:(n + 1) * 384, :] = out[:, h * 256:(h + 1) * 256]


def moment(near, far, ctx_t):
    return pl.pallas_call(
        moment_kernel,
        in_specs=vmem(3),
        out_specs=vmem(4),
        out_shape=[shape(768, 256)] * 4,
        scratch_shapes=[pltpu.VMEM((512, 2048), BF)],
        compiler_params=params(16),
        cost_estimate=cost(805_000_000, 4 * MIB),
        name="moment",
    )(near, far, ctx_t)


def context_grad_kernel(*refs):
    near, far, wenc, out, whole = refs[0], refs[1], refs[2], refs[-2], refs[-1]
    gather_rows(near, far, whole)
    out[...] = dot(whole[...], wenc[...], ((1,), (1,))).astype(BF)


def context_grad_of(near, far, wenc):
    return pl.pallas_call(
        context_grad_kernel,
        in_specs=vmem(3),
        out_specs=vmem(1)[0],
        out_shape=shape(512, 384),
        scratch_shapes=[pltpu.VMEM((512, 2048), BF)],
        compiler_params=params(16),
        cost_estimate=cost(805_000_000, 4 * MIB),
        name="context_grad",
    )(near, far, wenc)


def add_refs(*parts):
    return sum(p.astype(F32) for p in parts)


def second_x_kernel(a_keep, a_got, b_keep, b_got, after, a_send, b_send):
    a_send[...] = add_refs(a_keep[32:, :], a_got[32:, :]).astype(BF)
    b_send[...] = add_refs(b_keep[32:, :], b_got[32:, :]).astype(BF)


def second_x(a_keep, a_got, b_keep, b_got, after):
    return pl.pallas_call(
        second_x_kernel,
        in_specs=vmem(4) + any_space(1),
        out_specs=vmem(2),
        out_shape=[shape(32, 2048)] * 2,
        compiler_params=params(4),
        cost_estimate=cost(0, 1 * MIB),
        name="second_x",
    )(a_keep, a_got, b_keep, b_got, after)


def second_y_kernel(*refs):
    a_keep, a_got, a_last, b_keep, b_got, b_last = refs[:6]
    ma_keep, ma_got, mb_keep, mb_got, far, near, a_send, b_send = refs[6:]
    far[...] = add_refs(a_keep[:32, :], a_got[:32, :], a_last[...]).astype(BF)
    near[...] = add_refs(b_keep[:32, :], b_got[:32, :], b_last[...])
    a_send[...] = add_refs(ma_keep[384:, :], ma_got[384:, :]).astype(BF)
    b_send[...] = add_refs(mb_keep[384:, :], mb_got[384:, :]).astype(BF)


def second_y(*parts):
    return pl.pallas_call(
        second_y_kernel,
        in_specs=vmem(10),
        out_specs=vmem(4),
        out_shape=[shape(32, 2048), shape(32, 2048, dtype=F32)] + [shape(384, 256)] * 2,
        compiler_params=params(8),
        cost_estimate=cost(0, 2 * MIB),
        name="second_y",
    )(*parts)


def moment_sum_kernel(a_keep, a_got, a_last, b_keep, b_got, b_last, *outs):
    for n, refs in enumerate(((a_keep, a_got, a_last), (b_keep, b_got, b_last))):
        total = add_refs(refs[0][:384, :], refs[1][:384, :], refs[2][...]).astype(BF)
        outs[2 * n][...] = total[:, :128]
        outs[2 * n + 1][...] = total[:, 128:]


def moment_sum(*parts):
    return pl.pallas_call(
        moment_sum_kernel,
        in_specs=vmem(6),
        out_specs=vmem(4),
        out_shape=[shape(384, 128)] * 4,
        compiler_params=params(8),
        cost_estimate=cost(0, 2 * MIB),
        name="moment_sum",
    )(*parts)


def code_kernel(near, recv, after, code, *outs):
    code[...] = (near[...] + recv[...].astype(F32)).astype(BF)
    by_group(code, 128, outs)


def code_of(near, recv, after):
    return pl.pallas_call(
        code_kernel,
        in_specs=vmem(2) + any_space(1),
        out_specs=vmem(5),
        out_shape=[shape(32, 2048)] + [shape(32, 512)] * 4,
        compiler_params=params(8),
        cost_estimate=cost(0, 1 * MIB),
        name="code",
    )(near, recv, after)


def layer_out_kernel(code, dec, out):
    for g in range(GROUPS):
        out[:, g * 384:(g + 1) * 384] = dot(
            code[:, g * 128:(g + 1) * 128], dec[g * 128:(g + 1) * 128, :], ((1,), (0,))
        ).astype(BF)


def codec_grads_kernel(w_hbm, *refs):
    parts, codes, cots = refs[:4], refs[4:8], refs[8:12]
    total, own, other, enc_term, dec_term, w_block, sem = refs[12:]
    i, t = lax.axis_index("dp"), lax.axis_index("tensor")
    copy = pltpu.make_async_copy(w_hbm.at[:, ds(i, 384)], w_block, sem)
    copy.start()
    code = jnp.concatenate([r[...] for r in codes], axis=0)
    cot = jnp.concatenate([r[...] for r in cots], axis=0)
    dec_term[...] = dot(code, cot, ((0,), (0,)))
    total[...] = sum(r[...].astype(F32) for r in parts).astype(BF)
    copy.wait()
    enc_term[...] = dot(total[...], w_block[...], ((0,), (0,)))
    for dc, out in enumerate((own, other)):
        n = 0
        for dx in range(4):
            for dz in range(2):
                rows = ds(tadd(t, (dz, dx, dc)), 8)
                out[n:n + 8, :] = enc_term[rows, :]
                out[n + 8:n + 16, :] = dec_term[rows, :]
                n += 16


def w_out_grad_kernel(total, enc, out):
    i = lax.axis_index("dp")
    out[...] = dot(total[...], enc[ds(i, 128), :], ((1,), (0,)))


def add(*parts):
    return sum(p.astype(F32) for p in parts)


def on_device(ctx, w, enc, dec, cot):
    grad_code, *cots = pl.pallas_call(
        grad_code_kernel,
        in_specs=[pl.BlockSpec(memory_space=pltpu.HBM)] * 2,
        out_specs=vmem(5),
        out_shape=[shape(32, 2048)] + [shape(32, 1536)] * 4,
        scratch_shapes=[
            pltpu.VMEM((32, 6144), BF), pltpu.VMEM((2048, 384), BF),
            pltpu.SemaphoreType.DMA((5,)),
        ],
        compiler_params=pltpu.CompilerParams(vmem_limit_bytes=FIRST_VMEM),
        cost_estimate=cost(50_000_000, 2 * MIB),
        name="grad_code",
    )(cot, dec)

    theirs = fetch_tensor(grad_code, (1, 0, 0))
    cots = over_y(cots)
    wenc, ctx_t, ctx_r = wenc_of(w, ctx, enc, cots[1])

    own, other, pair, *cots = coded_of(ctx_r, wenc, grad_code, theirs, cots)
    pieces = [pair] + [fetch_tensor(pair, (0, k, 0)) for k in (1, 2, 3)]
    got = send_tensor(other, (0, 0, 1))
    cots = over_z(cots)

    packed, a_send, a_keep, b_send, b_keep = pack(pieces, own, got, *cots[1:])
    packed_far = send_tensor(packed, (0, 0, 1))
    a_got, b_got = swap_x(a_send, 1), swap_x(b_send, 3)

    ma_send, ma_keep, mb_send, mb_keep = moment(packed, packed_far, ctx_t)
    ma_got, mb_got = swap_y(ma_send, 1), swap_y(mb_send, 3)

    a_send, b_send = second_x(a_keep, a_got, b_keep, b_got, ma_send)
    a_last, b_last = swap_x(a_send, 3), swap_x(b_send, 1)

    far, near, a_send, b_send = second_y(
        a_keep, a_got, a_last, b_keep, b_got, b_last, ma_keep, ma_got, mb_keep, mb_got
    )
    recv = send_tensor(far, (1, 0, 0))
    ma_last, mb_last = swap_y(a_send, 3), swap_y(b_send, 1)

    subs = over_z(moment_sum(ma_keep, ma_got, ma_last, mb_keep, mb_got, mb_last))
    code, *codes = code_of(near, recv, subs[1])
    codes = over_z(code_regroup(over_y(codes)))

    context_grad = context_grad_of(packed, packed_far, wenc)
    layer_out = pl.pallas_call(
        layer_out_kernel,
        in_specs=vmem(2),
        out_specs=vmem(1)[0],
        out_shape=shape(32, 6144),
        compiler_params=params(8),
        cost_estimate=cost(50_000_000, 2 * MIB),
        name="layer_out",
    )(code, dec)

    total, own, other = pl.pallas_call(
        codec_grads_kernel,
        in_specs=[pl.BlockSpec(memory_space=pltpu.HBM)] + vmem(12),
        out_specs=vmem(3),
        out_shape=[shape(384, 128)] + [shape(128, 384, dtype=F32)] * 2,
        scratch_shapes=[
            pltpu.VMEM((128, 384), F32), pltpu.VMEM((128, 384), F32),
            pltpu.VMEM((384, 384), BF), pltpu.SemaphoreType.DMA,
        ],
        compiler_params=params(8),
        cost_estimate=cost(100_000_000, 2 * MIB),
        name="codec_grads",
    )(w, *subs, *codes, *cots)
    got = send_tensor(other, (0, 0, 1))
    part = [add(own[32 * k:32 * k + 32], got[32 * k:32 * k + 32]) for k in range(4)]
    rows = [part[0]] + [send_tensor(part[k], (0, k, 0)) for k in (2, 1, 3)]
    far = add(*[r[16:] for r in rows])
    near = add(*[r[:16] for r in rows])
    grads = near + send_tensor(far, (1, 0, 0))
    encoder_grad, decoder_grad = grads[:8], grads[8:]
    w_out_grad = pl.pallas_call(
        w_out_grad_kernel,
        in_specs=vmem(2),
        out_specs=vmem(1)[0],
        out_shape=shape(384, 384, dtype=F32),
        compiler_params=params(8),
        cost_estimate=cost(50_000_000, 2 * MIB),
        name="w_out_grad",
    )(total, enc)
    return layer_out, context_grad, w_out_grad, encoder_grad, decoder_grad


def solution(mesh):
    placed = (P("dp", "tensor"), P("tensor", None), P(), P(), P(("dp", "tensor"), None))
    return jax.shard_map(
        on_device,
        mesh=mesh,
        in_specs=placed,
        out_specs=(
            P(("dp", "tensor"), None),
            P("dp", "tensor"),
            P("tensor", "dp"),
            P(("dp", "tensor"), None),
            P(("dp", "tensor"), None),
        ),
        check_vma=False,
    )
```

time: 578 us -> 110 us (0.19)
  waiting for transfers between devices: 507 us -> 42.1 us
  starting transfers between devices: 0.34 us -> 48.6 us
  matrix products: 37.1 us -> 0 us
  Pallas kernels: 0 us -> 13.7 us
  between operations: 13.9 us -> 0.86 us
  local copies, waits for them, and re-layouts: 16.4 us -> 4.78 us
    unnamed x5 -> x0, waiting for transfers between devices: 248 us -> none
    reduce_scatter x2 -> x0, waiting for transfers between devices: 200 us -> none  [the longest x1 112 us: on_device(): lax.psum_scatter(weight_term.astype(jnp.bfloat16), 'dp', scatter_dimensio...]
    all_gather x1 -> x0, waiting for transfers between devices: 59.1 us -> none  [on_device(): lax.all_gather(grad_codes.reshape(local_rows, code_width), 'tensor', axis...]
    ppermute x0 -> x35, starting transfers between devices: none -> 48.6 us  [the longest x15 20.7 us: send_dp(): return lax.ppermute(v, 'dp', [(s, dp_add(s, rel)) for s in range(16)])]
    ppermute x0 -> x35, waiting for transfers between devices: none -> 42.1 us  [the longest x15 20.6 us: send_dp(): return lax.ppermute(v, 'dp', [(s, dp_add(s, rel)) for s in range(16)])]
    dot_general x9 -> x0, matrix products: 37.1 us -> none  [the longest x1 8.5 us: on_device(): lax.dot_general(back, w_out, (((1,), (1,)), ((), ())), preferred_element_...]
    pallas_call x0 -> x14, Pallas kernels: none -> 13.7 us  [the longest x1 2.9 us: on_device(): pl.pallas_call(grad_code_kernel, in_specs=[pl.BlockSpec(memory_space=pltp...]
  transfers between devices with their start and end apart: 4 -> 35, of which waited for: 4 -> 19; matrix products, arithmetic and copies ran while one was open for 4% -> 0% of each run, Pallas kernels for 0% -> 8%
where the time goes in v1:
time: 110 us
  starting transfers between devices  48.6 us (44%)
  waiting for transfers between devices  42.1 us (38%)
  Pallas kernels  13.7 us (12%)
  local copies, waits for them, and re-layouts  4.78 us (4%)
    ppermute x15, starting transfers between devices, send_dp(): return lax.ppermute(v, 'dp', [(s, dp_add(s, rel)) for s in range(16)])  20.7 us
    ppermute x15, waiting for transfers between devices, send_dp(): return lax.ppermute(v, 'dp', [(s, dp_add(s, rel)) for s in range(16)])  20.6 us
    ppermute x4, starting transfers between devices, fetch_tensor(): lax.ppermute(v, 'tensor', [(s, tensor_add(s, rel, -1)) for s in range(16)])  10.1 us
    ppermute x8, starting transfers between devices, send_tensor(): lax.ppermute(v, 'tensor', [(s, tensor_add(s, rel)) for s in range(16)])  8.89 us
    ppermute x8, waiting for transfers between devices, send_tensor(): lax.ppermute(v, 'tensor', [(s, tensor_add(s, rel)) for s in range(16)])  8.39 us
    ppermute x4, waiting for transfers between devices, swap_x(): return lax.ppermute(v, 'tensor', [(s, s ^ 2 * r) for s in range(16)])  8.21 us
    ppermute x4, starting transfers between devices, swap_y(): return lax.ppermute(v, 'dp', [(s, s ^ 4 * r) for s in range(16)])  5.54 us
    ppermute x4, waiting for transfers between devices, swap_y(): return lax.ppermute(v, 'dp', [(s, s ^ 4 * r) for s in range(16)])  4.88 us
  transfers between devices with their start and end apart: 35, of which 19 were waited for; matrix products, arithmetic and copies ran while one was open for 0% of the time, Pallas kernels for 8%

profile of v1, /device:TPU:30, one launch (start us, length us, event | category | flops | bytes accessed | tf_op | source)
XLA Modules:
  0.0 110.0 jit_solution(2836445392157505425)
XLA Ops:
  0.6 2.9 %grad_code.1 = (bf16[32,2048]{1,0:T(8,128)(2,1)}, bf16[32,1536]{1,0:T(8,128)(2,1)}, bf16[32,1536]{1,0:T(8,128)(2,1)}, bf16[32,1536]{1,0:T(8,128)(2,1)}, bf16[32,1536]{1,0:T(8,128)(2,1)}) custom-call(bf16[32,6144]{1,0:T(8,128)(2,1)} %cot_hbm.1, bf16[2048,384]{1,0:T(8,128)(2,1)} %dec.1), custom_call_target="tpu_custom_call" | custom-call | flops 50000000 | bytes 2097152 | tf_op jit(solution)/shard_map/grad_code/pallas_call | solution.py:410
  3.8 7.2 %collective-permute-start.1 = (bf16[32,2048]{1,0:T(8,128)(2,1)}, bf16[32,2048]{1,0:T(8,128)(2,1)S(1)}, u32[]{:S(2)}, u32[]{:S(2)}) collective-permute-start(bf16[32,2048]{1,0:T(8,128)(2,1)} %get-tuple-element.54.refs_2_), channel_id=1, source_target_pairs={{0,8},{1,9},{2,10},{3,11},{4,12},{5,13},{6,14},{7,15},{8,0},{9,1},... | collective-permute-start | bytes 393224 | tf_op jit(solution)/shard_map/ppermute | solution.py:34
  11.0 2.6 %collective-permute-start.2 = (bf16[32,1536]{1,0:T(8,128)(2,1)}, bf16[32,1536]{1,0:T(8,128)(2,1)S(1)}, u32[]{:S(2)}, u32[]{:S(2)}) collective-permute-start(bf16[32,1536]{1,0:T(8,128)(2,1)} %get-tuple-element.56), channel_id=1, source_target_pairs={{0,128},{16,144},{32,160},{48,176},{64,192},{80,208},{96,224},{112... | collective-permute-start | bytes 294920 | tf_op jit(solution)/shard_map/ppermute | solution.py:46
  13.6 2.3 %copy-done = bf16[384,6144]{1,0:T(8,128)(2,1)S(1)} copy-done((bf16[384,6144]{1,0:T(8,128)(2,1)S(1)}, bf16[384,6144]{1,0:T(8,128)(2,1)}, u32[]{:S(2)}) %copy-start) | copy-done | bytes 4718616
  16.0 1.4 %copy-done.1 = bf16[2048,384]{1,0:T(8,128)(2,1)S(1)} copy-done((bf16[2048,384]{1,0:T(8,128)(2,1)S(1)}, bf16[2048,384]{1,0:T(8,128)(2,1)}, u32[]{:S(2)}) %copy-start.1) | copy-done | bytes 1572888
  17.4 2.6 %wenc.1 = (bf16[384,2048]{1,0:T(8,128)(2,1)S(1)}, bf16[384,512]{1,0:T(8,128)(2,1)S(1)}, bf16[512,384]{1,0:T(8,128)(2,1)S(1)}) custom-call(bf16[384,6144]{1,0:T(8,128)(2,1)S(1)} %copy-done, bf16[512,384]{1,0:T(8,128)(2,1)S(1)} %copy-done.4, bf16[2048,384]{1,0:T(8,128)(2,1)S(1)} %copy-done.1, bf16[32,1536]{1,0:T(8,128)(2,1)S(1)} %collective-permute-done.after.refs_5_), custom_call_target="tpu_custom_call" | custom-call | flops 604000000 | bytes 9437184 | tf_op jit(solution)/shard_map/wenc/pallas_call | solution.py:175
  20.1 1.3 %coded.1 = (bf16[256,2048]{1,0:T(8,128)(2,1)S(1)}, bf16[256,2048]{1,0:T(8,128)(2,1)S(1)}, bf16[64,2048]{1,0:T(8,128)(2,1)S(1)}, bf16[128,384]{1,0:T(8,128)(2,1)S...) custom-call(bf16[512,384]{1,0:T(8,128)(2,1)S(1)} %get-tuple-element.52.refs_0_, ...), custom_call_target="tpu_custom_call" | custom-call | flops 805000000 | bytes 4194304 | tf_op jit(solution)/shard_map/coded/pallas_call | solution.py:201
  21.5 1.1 collective-permute-start.8
  23.1 2.4 %collective-permute-start.5 = (bf16[64,2048]{1,0:T(8,128)(2,1)S(1)}, bf16[64,2048]{1,0:T(8,128)(2,1)S(1)}, u32[]{:S(2)}, u32[]{:S(2)}) collective-permute-start(bf16[64,2048]{1,0:T(8,128)(2,1)S(1)} %get-tuple-element.58.refs_0_), channel_id=1, source_target_pairs={{0,4},{1,5},{2,6},{3,7},{4,0},{5,1},{6,2},{7,3},{8,12},{9,13},{10,... | collective-permute-start | bytes 786440 | tf_op jit(solution)/shard_map/ppermute | solution.py:34
  25.5 3.0 %collective-permute-done.8.refs_6_.refs_9_ = bf16[128,384]{1,0:T(8,128)(2,1)S(1)} collective-permute-done((bf16[128,384]{1,0:T(8,128)(2,1)S(1)}, bf16[128,384]{1,0:T(8,128)(2,1)S(1)}, u32[]{:S(2)}, u32[]{:S(2)}) %collective-permute-start.8) | collective-permute-done | bytes 98336 | tf_op jit(solution)/shard_map/ppermute | solution.py:46
  28.5 6.3 %collective-permute-done.9.refs_7_.refs_10_ = bf16[128,384]{1,0:T(8,128)(2,1)S(1)} collective-permute-done((bf16[128,384]{1,0:T(8,128)(2,1)S(1)}, bf16[128,384]{1,0:T(8,128)(2,1)S(1)}, u32[]{:S(2)}, u32[]{:S(2)}) %collective-permute-start.9) | collective-permute-done | bytes 98336 | tf_op jit(solution)/shard_map/ppermute | solution.py:46
  34.8 1.2 %collective-permute-start.10 = (bf16[128,384]{1,0:T(8,128)(2,1)S(1)}, bf16[128,384]{1,0:T(8,128)(2,1)S(1)}, u32[]{:S(2)}, u32[]{:S(2)}) collective-permute-start(bf16[128,384]{1,0:T(8,128)(2,1)S(1)} %get-tuple-element.63), channel_id=1, source_target_pairs={{0,48},{16,0},{32,16},{48,32},{64,112},{80,64},{96,80},{112,96},{1... | collective-permute-start | bytes 294920 | tf_op jit(solution)/shard_map/ppermute | solution.py:46
  36.0 3.4 %collective-permute-done.10.refs_8_.refs_11_ = bf16[128,384]{1,0:T(8,128)(2,1)S(1)} collective-permute-done((bf16[128,384]{1,0:T(8,128)(2,1)S(1)}, bf16[128,384]{1,0:T(8,128)(2,1)S(1)}, u32[]{:S(2)}, u32[]{:S(2)}) %collective-permute-start.10) | collective-permute-done | bytes 98336 | tf_op jit(solution)/shard_map/ppermute | solution.py:46
  39.8 0.9 collective-permute-start.11
  40.8 1.2 %collective-permute-start.12 = (bf16[64,2048]{1,0:T(8,128)(2,1)S(1)}, bf16[64,2048]{1,0:T(8,128)(2,1)S(1)}, u32[]{:S(2)}, u32[]{:S(2)}) collective-permute-start(bf16[64,2048]{1,0:T(8,128)(2,1)S(1)} %get-tuple-element.67), channel_id=1, source_target_pairs={{0,6},{1,7},{2,4},{3,5},{4,2},{5,3},{6,0},{7,1},{8,14},{9,15},{10,... | collective-permute-start | bytes 786440 | tf_op jit(solution)/shard_map/ppermute | solution.py:38
  42.5 1.2 %moment.1 = (bf16[768,256]{1,0:T(8,128)(2,1)S(1)}, bf16[768,256]{1,0:T(8,128)(2,1)S(1)}, bf16[768,256]{1,0:T(8,128)(2,1)S(1)}, bf16[768,256]{1,0:T(8,128)(2,1)S(1)}) custom-call(bf16[256,2048]{1,0:T(8,128)(2,1)S(1)} %get-tuple-element.68.near.refs_0_, bf16[256,2048]{1,0:T(8,128)(2,1)S(1)} %collective-permute-done.13.far.refs_1_, ...), custom_call_target="tpu_custom_call" | custom-call | flops 805000000 | bytes 4194304 | tf_op jit(solution)/shard_map/moment/pallas_call | solution.py:262
  43.7 3.3 %collective-permute-start.17 = (bf16[768,256]{1,0:T(8,128)(2,1)S(1)}, bf16[768,256]{1,0:T(8,128)(2,1)S(1)}, u32[]{:S(2)}, u32[]{:S(2)}) collective-permute-start(bf16[768,256]{1,0:T(8,128)(2,1)S(1)} %get-tuple-element.75), channel_id=1, source_target_pairs={{0,192},{16,208},{32,224},{48,240},{64,128},{80,144},{96,160},{112... | collective-permute-start | bytes 1179656 | tf_op jit(solution)/shard_map/ppermute | solution.py:42
  47.1 1.5 %collective-permute-done.11.a_got.refs_1_ = bf16[64,2048]{1,0:T(8,128)(2,1)S(1)} collective-permute-done((bf16[64,2048]{1,0:T(8,128)(2,1)S(1)}, bf16[64,2048]{1,0:T(8,128)(2,1)S(1)}, u32[]{:S(2)}, u32[]{:S(2)}) %collective-permute-start.11) | collective-permute-done | bytes 262176 | tf_op jit(solution)/shard_map/ppermute | solution.py:38
  48.6 1.8 %collective-permute-done.12.b_got.refs_4_ = bf16[64,2048]{1,0:T(8,128)(2,1)S(1)} collective-permute-done((bf16[64,2048]{1,0:T(8,128)(2,1)S(1)}, bf16[64,2048]{1,0:T(8,128)(2,1)S(1)}, u32[]{:S(2)}, u32[]{:S(2)}) %collective-permute-start.12) | collective-permute-done | bytes 262176 | tf_op jit(solution)/shard_map/ppermute | solution.py:38
  50.4 1.3 %collective-permute-start.14 = (bf16[32,2048]{1,0:T(8,128)(2,1)S(1)}, bf16[32,2048]{1,0:T(8,128)(2,1)S(1)}, u32[]{:S(2)}, u32[]{:S(2)}) collective-permute-start(bf16[32,2048]{1,0:T(8,128)(2,1)S(1)} %get-tuple-element.71), channel_id=1, source_target_pairs={{0,6},{1,7},{2,4},{3,5},{4,2},{5,3},{6,0},{7,1},{8,14},{9,15},{10,... | collective-permute-start | bytes 393224 | tf_op jit(solution)/shard_map/ppermute | solution.py:38
  51.7 5.0 %collective-permute-done.14.refs_2_ = bf16[32,2048]{1,0:T(8,128)(2,1)S(1)} collective-permute-done((bf16[32,2048]{1,0:T(8,128)(2,1)S(1)}, bf16[32,2048]{1,0:T(8,128)(2,1)S(1)}, u32[]{:S(2)}, u32[]{:S(2)}) %collective-permute-start.14) | collective-permute-done | bytes 131104 | tf_op jit(solution)/shard_map/ppermute | solution.py:38
  56.7 1.3 %collective-permute-done.16.refs_7_.a_got = bf16[768,256]{1,0:T(8,128)(2,1)S(1)} collective-permute-done((bf16[768,256]{1,0:T(8,128)(2,1)S(1)}, bf16[768,256]{1,0:T(8,128)(2,1)S(1)}, u32[]{:S(2)}, u32[]{:S(2)}) %collective-permute-start.16) | collective-permute-done | bytes 393248 | tf_op jit(solution)/shard_map/ppermute | solution.py:42
  58.1 2.1 %collective-permute-start.19 = (bf16[384,256]{1,0:T(8,128)(2,1)S(1)}, bf16[384,256]{1,0:T(8,128)(2,1)S(1)}, u32[]{:S(2)}, u32[]{:S(2)}) collective-permute-start(bf16[384,256]{1,0:T(8,128)(2,1)S(1)} %get-tuple-element.78), channel_id=1, source_target_pairs={{0,192},{16,208},{32,224},{48,240},{64,128},{80,144},{96,160},{112... | collective-permute-start | bytes 589832 | tf_op jit(solution)/shard_map/ppermute | solution.py:42
  60.2 2.0 %collective-permute-start.18 = (bf16[32,2048]{1,0:T(8,128)(2,1)S(1)}, bf16[32,2048]{1,0:T(8,128)(2,1)S(1)}, u32[]{:S(2)}, u32[]{:S(2)}) collective-permute-start(bf16[32,2048]{1,0:T(8,128)(2,1)S(1)} %get-tuple-element.77), channel_id=1, source_target_pairs={{0,8},{1,9},{2,10},{3,11},{4,12},{5,13},{6,14},{7,15},{8,0},{9,1},... | collective-permute-start | bytes 393224 | tf_op jit(solution)/shard_map/ppermute | solution.py:30
  62.2 3.0 %collective-permute-done.19.a_last = bf16[384,256]{1,0:T(8,128)(2,1)S(1)} collective-permute-done((bf16[384,256]{1,0:T(8,128)(2,1)S(1)}, bf16[384,256]{1,0:T(8,128)(2,1)S(1)}, u32[]{:S(2)}, u32[]{:S(2)}) %collective-permute-start.19) | collective-permute-done | bytes 196640 | tf_op jit(solution)/shard_map/ppermute | solution.py:42
  65.2 0.7 collective-permute-done.20.b_last
  66.2 4.4 %collective-permute-start.22 = (bf16[384,128]{1,0:T(8,128)(2,1)S(1)}, bf16[384,128]{1,0:T(8,128)(2,1)S(1)}, u32[]{:S(2)}, u32[]{:S(2)}) collective-permute-start(bf16[384,128]{1,0:T(8,128)(2,1)S(1)} %get-tuple-element.83), channel_id=1, source_target_pairs={{0,32},{16,48},{32,0},{48,16},{64,96},{80,112},{96,64},{112,80},{1... | collective-permute-start | bytes 294920 | tf_op jit(solution)/shard_map/ppermute | solution.py:46
  70.6 1.1 collective-permute-done.18.recv
  71.7 2.1 %collective-permute-done.21.after.refs_1_ = bf16[384,128]{1,0:T(8,128)(2,1)S(1)} collective-permute-done((bf16[384,128]{1,0:T(8,128)(2,1)S(1)}, bf16[384,128]{1,0:T(8,128)(2,1)S(1)}, u32[]{:S(2)}, u32[]{:S(2)}) %collective-permute-start.21) | collective-permute-done | bytes 98336 | tf_op jit(solution)/shard_map/ppermute | solution.py:46
  73.8 1.3 %collective-permute-start.24 = (bf16[32,512]{1,0:T(8,128)(2,1)S(1)}, bf16[32,512]{1,0:T(8,128)(2,1)S(1)}, u32[]{:S(2)}, u32[]{:S(2)}) collective-permute-start(bf16[32,512]{1,0:T(8,128)(2,1)S(1)} %get-tuple-element.86), channel_id=1, source_target_pairs={{0,64},{16,80},{32,96},{48,112},{64,128},{80,144},{96,160},{112,17... | collective-permute-start | bytes 98312 | tf_op jit(solution)/shard_map/ppermute | solution.py:46
  75.1 1.8 %collective-permute-start.25 = (bf16[32,512]{1,0:T(8,128)(2,1)S(1)}, bf16[32,512]{1,0:T(8,128)(2,1)S(1)}, u32[]{:S(2)}, u32[]{:S(2)}) collective-permute-start(bf16[32,512]{1,0:T(8,128)(2,1)S(1)} %get-tuple-element.87), channel_id=1, source_target_pairs={{0,128},{16,144},{32,160},{48,176},{64,192},{80,208},{96,224},{112... | collective-permute-start | bytes 98312 | tf_op jit(solution)/shard_map/ppermute | solution.py:46
  76.9 0.9 collective-permute-start.26
  77.9 2.7 %collective-permute-done.25.refs_2_ = bf16[32,512]{1,0:T(8,128)(2,1)S(1)} collective-permute-done((bf16[32,512]{1,0:T(8,128)(2,1)S(1)}, bf16[32,512]{1,0:T(8,128)(2,1)S(1)}, u32[]{:S(2)}, u32[]{:S(2)}) %collective-permute-start.25) | collective-permute-done | bytes 32800 | tf_op jit(solution)/shard_map/ppermute | solution.py:46
  80.5 1.5 %collective-permute-done.26.refs_3_ = bf16[32,512]{1,0:T(8,128)(2,1)S(1)} collective-permute-done((bf16[32,512]{1,0:T(8,128)(2,1)S(1)}, bf16[32,512]{1,0:T(8,128)(2,1)S(1)}, u32[]{:S(2)}, u32[]{:S(2)}) %collective-permute-start.26) | collective-permute-done | bytes 32800 | tf_op jit(solution)/shard_map/ppermute | solution.py:46
  82.1 2.0 %collective-permute-start.27 = (bf16[128,128]{1,0:T(8,128)(2,1)S(1)}, bf16[128,128]{1,0:T(8,128)(2,1)S(1)}, u32[]{:S(2)}, u32[]{:S(2)}) collective-permute-start(bf16[128,128]{1,0:T(8,128)(2,1)S(1)} %get-tuple-element.90), channel_id=1, source_target_pairs={{0,16},{16,32},{32,48},{48,0},{64,80},{80,96},{96,112},{112,64},{1... | collective-permute-start | bytes 98312 | tf_op jit(solution)/shard_map/ppermute | solution.py:46
  84.1 2.0 %collective-permute-start.28 = (bf16[128,128]{1,0:T(8,128)(2,1)S(1)}, bf16[128,128]{1,0:T(8,128)(2,1)S(1)}, u32[]{:S(2)}, u32[]{:S(2)}) collective-permute-start(bf16[128,128]{1,0:T(8,128)(2,1)S(1)} %get-tuple-element.91), channel_id=1, source_target_pairs={{0,32},{16,48},{32,0},{48,16},{64,96},{80,112},{96,64},{112,80},{1... | collective-permute-start | bytes 98312 | tf_op jit(solution)/shard_map/ppermute | solution.py:46
  86.1 2.8 %collective-permute-start.29 = (bf16[128,128]{1,0:T(8,128)(2,1)S(1)}, bf16[128,128]{1,0:T(8,128)(2,1)S(1)}, u32[]{:S(2)}, u32[]{:S(2)}) collective-permute-start(bf16[128,128]{1,0:T(8,128)(2,1)S(1)} %get-tuple-element.92), channel_id=1, source_target_pairs={{0,48},{16,0},{32,16},{48,32},{64,112},{80,64},{96,80},{112,96},{1... | collective-permute-start | bytes 98312 | tf_op jit(solution)/shard_map/ppermute | solution.py:46
  88.9 1.6 %collective-permute-done.29.refs_7_ = bf16[128,128]{1,0:T(8,128)(2,1)S(1)} collective-permute-done((bf16[128,128]{1,0:T(8,128)(2,1)S(1)}, bf16[128,128]{1,0:T(8,128)(2,1)S(1)}, u32[]{:S(2)}, u32[]{:S(2)}) %collective-permute-start.29) | collective-permute-done | bytes 32800 | tf_op jit(solution)/shard_map/ppermute | solution.py:46
  91.2 1.4 %collective-permute-done.30 = f32[128,384]{1,0:T(8,128)S(1)} collective-permute-done((f32[128,384]{1,0:T(8,128)S(1)}, f32[128,384]{1,0:T(8,128)S(1)}, u32[]{:S(2)}, u32[]{:S(2)}) %collective-permute-start.30) | collective-permute-done | bytes 196640 | tf_op jit(solution)/shard_map/ppermute | solution.py:30
  92.7 0.9 collective-permute-start.33
  93.6 2.4 %collective-permute-start.32 = (f32[32,384]{1,0:T(8,128)S(1)}, f32[32,384]{1,0:T(8,128)S(1)}, u32[]{:S(2)}, u32[]{:S(2)}) collective-permute-start(f32[32,384]{1,0:T(8,128)S(1)} %get-tuple-element.99), channel_id=1, source_target_pairs={{0,2},{1,3},{2,4},{3,5},{4,6},{5,7},{6,0},{7,1},{8,10},{9,11},{10,... | collective-permute-start | bytes 147464 | tf_op jit(solution)/shard_map/ppermute | solution.py:30
  96.5 1.5 %collective-permute-done.33 = f32[32,384]{1,0:T(8,128)S(1)} collective-permute-done((f32[32,384]{1,0:T(8,128)S(1)}, f32[32,384]{1,0:T(8,128)S(1)}, u32[]{:S(2)}, u32[]{:S(2)}) %collective-permute-start.33) | collective-permute-done | bytes 49184 | tf_op jit(solution)/shard_map/ppermute | solution.py:30
  98.0 3.5 %collective-permute-done.31 = f32[32,384]{1,0:T(8,128)S(1)} collective-permute-done((f32[32,384]{1,0:T(8,128)S(1)}, f32[32,384]{1,0:T(8,128)S(1)}, u32[]{:S(2)}, u32[]{:S(2)}) %collective-permute-start.31) | collective-permute-done | bytes 49184 | tf_op jit(solution)/shard_map/ppermute | solution.py:30
  101.6 2.8 %collective-permute-start.34 = (f32[16,384]{1,0:T(8,128)S(1)}, f32[16,384]{1,0:T(8,128)S(1)}, u32[]{:S(2)}, u32[]{:S(2)}) collective-permute-start(f32[16,384]{1,0:T(8,128)S(1)} %slice_add_fusion.4), channel_id=1, source_target_pairs={{0,8},{1,9},{2,10},{3,11},{4,12},{5,13},{6,14},{7,15},{8,0},{9,1},... | collective-permute-start | bytes 73736 | tf_op jit(solution)/shard_map/ppermute | solution.py:30
  104.4 2.1 %context_grad.1 = bf16[512,384]{1,0:T(8,128)(2,1)} custom-call(bf16[256,2048]{1,0:T(8,128)(2,1)S(1)} %get-tuple-element.68.near.refs_0_, bf16[256,2048]{1,0:T(8,128)(2,1)S(1)} %collective-permute-done.13.far.refs_1_, bf16[384,2048]{1,0:T(8,128)(2,1)S(1)} %get-tuple-element.53.refs_1_.refs_2_), custom_call_target="tpu_custom_call" | custom-call | flops 805000000 | bytes 4194304 | tf_op jit(solution)/shard_map/context_grad/pallas_call | solution.py:281
  106.5 1.1 %layer_out.1 = bf16[32,6144]{1,0:T(8,128)(2,1)} custom-call(bf16[32,2048]{1,0:T(8,128)(2,1)S(1)} %get-tuple-element.81.code, bf16[2048,384]{1,0:T(8,128)(2,1)S(1)} %copy-done.3), custom_call_target="tpu_custom_call" | custom-call | flops 50000000 | bytes 2097152 | tf_op jit(solution)/shard_map/layer_out/pallas_call | solution.py:454
  108.1 1.0 w_out_grad.1
  109.4 0.6 fusion.1
  (59 shorter events, 4.7 us)
Async XLA Ops:
  0.6 13.0 %copy-start.4 = (bf16[512,384]{1,0:T(8,128)(2,1)S(1)}, bf16[512,384]{1,0:T(8,128)(2,1)}, u32[]{:S(2)}) copy-start(bf16[512,384]{1,0:T(8,128)(2,1)} %ctx.1) | copy-start | bytes 1179652
  3.5 10.1 %collective-permute-start = (bf16[32,1536]{1,0:T(8,128)(2,1)}, bf16[32,1536]{1,0:T(8,128)(2,1)S(1)}, u32[]{:S(2)}, u32[]{:S(2)}) collective-permute-start(bf16[32,1536]{1,0:T(8,128)(2,1)} %get-tuple-element.51), channel_id=1, source_target_pairs={{0,64},{16,80},{32,96},{48,112},{64,128},{80,144},{96,160},{112,17... | collective-permute-start | bytes 294920 | tf_op jit(solution)/shard_map/ppermute | solution.py:46
  3.8 16.2 %collective-permute-start.1 = (bf16[32,2048]{1,0:T(8,128)(2,1)}, bf16[32,2048]{1,0:T(8,128)(2,1)S(1)}, u32[]{:S(2)}, u32[]{:S(2)}) collective-permute-start(bf16[32,2048]{1,0:T(8,128)(2,1)} %get-tuple-element.54.refs_2_), channel_id=1, source_target_pairs={{0,8},{1,9},{2,10},{3,11},{4,12},{5,13},{6,14},{7,15},{8,0},{9,1},... | collective-permute-start | bytes 393224 | tf_op jit(solution)/shard_map/ppermute | solution.py:34
  11.0 9.0 %collective-permute-start.2 = (bf16[32,1536]{1,0:T(8,128)(2,1)}, bf16[32,1536]{1,0:T(8,128)(2,1)S(1)}, u32[]{:S(2)}, u32[]{:S(2)}) collective-permute-start(bf16[32,1536]{1,0:T(8,128)(2,1)} %get-tuple-element.56), channel_id=1, source_target_pairs={{0,128},{16,144},{32,160},{48,176},{64,192},{80,208},{96,224},{112... | collective-permute-start | bytes 294920 | tf_op jit(solution)/shard_map/ppermute | solution.py:46
  13.6 6.4 %collective-permute-start.3 = (bf16[32,1536]{1,0:T(8,128)(2,1)}, bf16[32,1536]{1,0:T(8,128)(2,1)S(1)}, u32[]{:S(2)}, u32[]{:S(2)}) collective-permute-start(bf16[32,1536]{1,0:T(8,128)(2,1)} %get-tuple-element.57), channel_id=1, source_target_pairs={{0,192},{16,208},{32,224},{48,240},{64,0},{80,16},{96,32},{112,48}... | collective-permute-start | bytes 294920 | tf_op jit(solution)/shard_map/ppermute | solution.py:46
  13.6 2.3 %copy-start = (bf16[384,6144]{1,0:T(8,128)(2,1)S(1)}, bf16[384,6144]{1,0:T(8,128)(2,1)}, u32[]{:S(2)}) copy-start(bf16[384,6144]{1,0:T(8,128)(2,1)} %w_hbm.3) | copy-start | bytes 14155780
  16.0 1.4 %copy-start.1 = (bf16[2048,384]{1,0:T(8,128)(2,1)S(1)}, bf16[2048,384]{1,0:T(8,128)(2,1)}, u32[]{:S(2)}) copy-start(bf16[2048,384]{1,0:T(8,128)(2,1)} %enc.3) | copy-start | bytes 4718596
  17.4 2.7 %copy-start.5 = (bf16[32,2048]{1,0:T(8,128)(2,1)S(1)}, bf16[32,2048]{1,0:T(8,128)(2,1)}, u32[]{:S(2)}) copy-start(bf16[32,2048]{1,0:T(8,128)(2,1)} %get-tuple-element.54.refs_2_) | copy-start | bytes 393220
  17.4 2.7 %copy-start.6 = (bf16[32,1536]{1,0:T(8,128)(2,1)S(1)}, bf16[32,1536]{1,0:T(8,128)(2,1)}, u32[]{:S(2)}) copy-start(bf16[32,1536]{1,0:T(8,128)(2,1)} %get-tuple-element.55.refs_4_) | copy-start | bytes 294916
  20.1 70.5 %slice-start = ((s8[4718592]{0:T(1024)(128)(4,1)}), s8[524288]{0:T(1024)(128)(4,1)S(1)}, s32[]{:S(2)}) async-start(s8[4718592]{0:T(1024)(128)(4,1)} %bitcast), calls=%async_computation | async-start | bytes 1048576
  21.4 18.0 %collective-permute-start.7 = (bf16[256,2048]{1,0:T(8,128)(2,1)S(1)}, bf16[256,2048]{1,0:T(8,128)(2,1)S(1)}, u32[]{:S(2)}, u32[]{:S(2)}) collective-permute-start(bf16[256,2048]{1,0:T(8,128)(2,1)S(1)} %get-tuple-element.60), channel_id=1, source_target_pairs={{0,1},{1,0},{2,3},{3,2},{4,5},{5,4},{6,7},{7,6},{8,9},{9,8},{10,11... | collective-permute-start | bytes 3145736 | tf_op jit(solution)/shard_map/ppermute | solution.py:30
  21.5 7.0 %collective-permute-start.8 = (bf16[128,384]{1,0:T(8,128)(2,1)S(1)}, bf16[128,384]{1,0:T(8,128)(2,1)S(1)}, u32[]{:S(2)}, u32[]{:S(2)}) collective-permute-start(bf16[128,384]{1,0:T(8,128)(2,1)S(1)} %get-tuple-element.61), channel_id=1, source_target_pairs={{0,16},{16,32},{32,48},{48,0},{64,80},{80,96},{96,112},{112,64},{1... | collective-permute-start | bytes 294920 | tf_op jit(solution)/shard_map/ppermute | solution.py:46
  22.6 16.8 %collective-permute-start.6 = (bf16[64,2048]{1,0:T(8,128)(2,1)S(1)}, bf16[64,2048]{1,0:T(8,128)(2,1)S(1)}, u32[]{:S(2)}, u32[]{:S(2)}) collective-permute-start(bf16[64,2048]{1,0:T(8,128)(2,1)S(1)} %get-tuple-element.58.refs_0_), channel_id=1, source_target_pairs={{0,2},{1,3},{2,4},{3,5},{4,6},{5,7},{6,0},{7,1},{8,10},{9,11},{10,... | collective-permute-start | bytes 786440 | tf_op jit(solution)/shard_map/ppermute | solution.py:34
  23.1 16.3 %collective-permute-start.5 = (bf16[64,2048]{1,0:T(8,128)(2,1)S(1)}, bf16[64,2048]{1,0:T(8,128)(2,1)S(1)}, u32[]{:S(2)}, u32[]{:S(2)}) collective-permute-start(bf16[64,2048]{1,0:T(8,128)(2,1)S(1)} %get-tuple-element.58.refs_0_), channel_id=1, source_target_pairs={{0,4},{1,5},{2,6},{3,7},{4,0},{5,1},{6,2},{7,3},{8,12},{9,13},{10,... | collective-permute-start | bytes 786440 | tf_op jit(solution)/shard_map/ppermute | solution.py:34
  25.5 13.9 %collective-permute-start.4 = (bf16[64,2048]{1,0:T(8,128)(2,1)S(1)}, bf16[64,2048]{1,0:T(8,128)(2,1)S(1)}, u32[]{:S(2)}, u32[]{:S(2)}) collective-permute-start(bf16[64,2048]{1,0:T(8,128)(2,1)S(1)} %get-tuple-element.58.refs_0_), channel_id=1, source_target_pairs={{0,6},{1,7},{2,0},{3,1},{4,2},{5,3},{6,4},{7,5},{8,14},{9,15},{10,... | collective-permute-start | bytes 786440 | tf_op jit(solution)/shard_map/ppermute | solution.py:34
  28.5 6.3 %collective-permute-start.9 = (bf16[128,384]{1,0:T(8,128)(2,1)S(1)}, bf16[128,384]{1,0:T(8,128)(2,1)S(1)}, u32[]{:S(2)}, u32[]{:S(2)}) collective-permute-start(bf16[128,384]{1,0:T(8,128)(2,1)S(1)} %get-tuple-element.62), channel_id=1, source_target_pairs={{0,32},{16,48},{32,0},{48,16},{64,96},{80,112},{96,64},{112,80},{1... | collective-permute-start | bytes 294920 | tf_op jit(solution)/shard_map/ppermute | solution.py:46
  34.8 4.6 %collective-permute-start.10 = (bf16[128,384]{1,0:T(8,128)(2,1)S(1)}, bf16[128,384]{1,0:T(8,128)(2,1)S(1)}, u32[]{:S(2)}, u32[]{:S(2)}) collective-permute-start(bf16[128,384]{1,0:T(8,128)(2,1)S(1)} %get-tuple-element.63), channel_id=1, source_target_pairs={{0,48},{16,0},{32,16},{48,32},{64,112},{80,64},{96,80},{112,96},{1... | collective-permute-start | bytes 294920 | tf_op jit(solution)/shard_map/ppermute | solution.py:46
  39.7 2.7 %collective-permute-start.13 = (bf16[256,2048]{1,0:T(8,128)(2,1)S(1)}, bf16[256,2048]{1,0:T(8,128)(2,1)S(1)}, u32[]{:S(2)}, u32[]{:S(2)}) collective-permute-start(bf16[256,2048]{1,0:T(8,128)(2,1)S(1)} %get-tuple-element.68.near.refs_0_), channel_id=1, source_target_pairs={{0,1},{1,0},{2,3},{3,2},{4,5},{5,4},{6,7},{7,6},{8,9},{9,8},{10,11... | collective-permute-start | bytes 3145736 | tf_op jit(solution)/shard_map/ppermute | solution.py:30
  39.8 8.7 %collective-permute-start.11 = (bf16[64,2048]{1,0:T(8,128)(2,1)S(1)}, bf16[64,2048]{1,0:T(8,128)(2,1)S(1)}, u32[]{:S(2)}, u32[]{:S(2)}) collective-permute-start(bf16[64,2048]{1,0:T(8,128)(2,1)S(1)} %get-tuple-element.65), channel_id=1, source_target_pairs={{0,2},{1,3},{2,0},{3,1},{4,6},{5,7},{6,4},{7,5},{8,10},{9,11},{10,... | collective-permute-start | bytes 786440 | tf_op jit(solution)/shard_map/ppermute | solution.py:38
  40.8 9.6 %collective-permute-start.12 = (bf16[64,2048]{1,0:T(8,128)(2,1)S(1)}, bf16[64,2048]{1,0:T(8,128)(2,1)S(1)}, u32[]{:S(2)}, u32[]{:S(2)}) collective-permute-start(bf16[64,2048]{1,0:T(8,128)(2,1)S(1)} %get-tuple-element.67), channel_id=1, source_target_pairs={{0,6},{1,7},{2,4},{3,5},{4,2},{5,3},{6,0},{7,1},{8,14},{9,15},{10,... | collective-permute-start | bytes 786440 | tf_op jit(solution)/shard_map/ppermute | solution.py:38
  42.5 48.0 %slice-start.1 = ((s8[4718592]{0:T(1024)(128)(4,1)}), s8[4194304]{0:T(1024)(128)(4,1)S(1)}, s32[]{:S(2)}) async-start(s8[4718592]{0:T(1024)(128)(4,1)} %bitcast), calls=%async_computation.1 | async-start | bytes 8388608
  43.7 12.9 %collective-permute-start.17 = (bf16[768,256]{1,0:T(8,128)(2,1)S(1)}, bf16[768,256]{1,0:T(8,128)(2,1)S(1)}, u32[]{:S(2)}, u32[]{:S(2)}) collective-permute-start(bf16[768,256]{1,0:T(8,128)(2,1)S(1)} %get-tuple-element.75), channel_id=1, source_target_pairs={{0,192},{16,208},{32,224},{48,240},{64,128},{80,144},{96,160},{112... | collective-permute-start | bytes 1179656 | tf_op jit(solution)/shard_map/ppermute | solution.py:42
  47.0 10.9 %collective-permute-start.16 = (bf16[768,256]{1,0:T(8,128)(2,1)S(1)}, bf16[768,256]{1,0:T(8,128)(2,1)S(1)}, u32[]{:S(2)}, u32[]{:S(2)}) collective-permute-start(bf16[768,256]{1,0:T(8,128)(2,1)S(1)} %get-tuple-element.70.after), channel_id=1, source_target_pairs={{0,64},{16,80},{32,96},{48,112},{64,0},{80,16},{96,32},{112,48},{1... | collective-permute-start | bytes 1179656 | tf_op jit(solution)/shard_map/ppermute | solution.py:42
  50.4 6.3 %collective-permute-start.14 = (bf16[32,2048]{1,0:T(8,128)(2,1)S(1)}, bf16[32,2048]{1,0:T(8,128)(2,1)S(1)}, u32[]{:S(2)}, u32[]{:S(2)}) collective-permute-start(bf16[32,2048]{1,0:T(8,128)(2,1)S(1)} %get-tuple-element.71), channel_id=1, source_target_pairs={{0,6},{1,7},{2,4},{3,5},{4,2},{5,3},{6,0},{7,1},{8,14},{9,15},{10,... | collective-permute-start | bytes 393224 | tf_op jit(solution)/shard_map/ppermute | solution.py:38
  51.7 5.0 %collective-permute-start.15 = (bf16[32,2048]{1,0:T(8,128)(2,1)S(1)}, bf16[32,2048]{1,0:T(8,128)(2,1)S(1)}, u32[]{:S(2)}, u32[]{:S(2)}) collective-permute-start(bf16[32,2048]{1,0:T(8,128)(2,1)S(1)} %get-tuple-element.72), channel_id=1, source_target_pairs={{0,2},{1,3},{2,0},{3,1},{4,6},{5,7},{6,4},{7,5},{8,10},{9,11},{10,... | collective-permute-start | bytes 393224 | tf_op jit(solution)/shard_map/ppermute | solution.py:38
  58.1 7.1 %collective-permute-start.19 = (bf16[384,256]{1,0:T(8,128)(2,1)S(1)}, bf16[384,256]{1,0:T(8,128)(2,1)S(1)}, u32[]{:S(2)}, u32[]{:S(2)}) collective-permute-start(bf16[384,256]{1,0:T(8,128)(2,1)S(1)} %get-tuple-element.78), channel_id=1, source_target_pairs={{0,192},{16,208},{32,224},{48,240},{64,128},{80,144},{96,160},{112... | collective-permute-start | bytes 589832 | tf_op jit(solution)/shard_map/ppermute | solution.py:42
  60.2 5.7 %collective-permute-start.20 = (bf16[384,256]{1,0:T(8,128)(2,1)S(1)}, bf16[384,256]{1,0:T(8,128)(2,1)S(1)}, u32[]{:S(2)}, u32[]{:S(2)}) collective-permute-start(bf16[384,256]{1,0:T(8,128)(2,1)S(1)} %get-tuple-element.79), channel_id=1, source_target_pairs={{0,64},{16,80},{32,96},{48,112},{64,0},{80,16},{96,32},{112,48},{1... | collective-permute-start | bytes 589832 | tf_op jit(solution)/shard_map/ppermute | solution.py:42
  60.2 11.4 %collective-permute-start.18 = (bf16[32,2048]{1,0:T(8,128)(2,1)S(1)}, bf16[32,2048]{1,0:T(8,128)(2,1)S(1)}, u32[]{:S(2)}, u32[]{:S(2)}) collective-permute-start(bf16[32,2048]{1,0:T(8,128)(2,1)S(1)} %get-tuple-element.77), channel_id=1, source_target_pairs={{0,8},{1,9},{2,10},{3,11},{4,12},{5,13},{6,14},{7,15},{8,0},{9,1},... | collective-permute-start | bytes 393224 | tf_op jit(solution)/shard_map/ppermute | solution.py:30
  66.0 7.8 %collective-permute-start.21 = (bf16[384,128]{1,0:T(8,128)(2,1)S(1)}, bf16[384,128]{1,0:T(8,128)(2,1)S(1)}, u32[]{:S(2)}, u32[]{:S(2)}) collective-permute-start(bf16[384,128]{1,0:T(8,128)(2,1)S(1)} %get-tuple-element.80), channel_id=1, source_target_pairs={{0,16},{16,32},{32,48},{48,0},{64,80},{80,96},{96,112},{112,64},{1... | collective-permute-start | bytes 294920 | tf_op jit(solution)/shard_map/ppermute | solution.py:46
  66.2 22.7 %collective-permute-start.22 = (bf16[384,128]{1,0:T(8,128)(2,1)S(1)}, bf16[384,128]{1,0:T(8,128)(2,1)S(1)}, u32[]{:S(2)}, u32[]{:S(2)}) collective-permute-start(bf16[384,128]{1,0:T(8,128)(2,1)S(1)} %get-tuple-element.83), channel_id=1, source_target_pairs={{0,32},{16,48},{32,0},{48,16},{64,96},{80,112},{96,64},{112,80},{1... | collective-permute-start | bytes 294920 | tf_op jit(solution)/shard_map/ppermute | solution.py:46
  70.6 18.3 %collective-permute-start.23 = (bf16[384,128]{1,0:T(8,128)(2,1)S(1)}, bf16[384,128]{1,0:T(8,128)(2,1)S(1)}, u32[]{:S(2)}, u32[]{:S(2)}) collective-permute-start(bf16[384,128]{1,0:T(8,128)(2,1)S(1)} %get-tuple-element.84), channel_id=1, source_target_pairs={{0,48},{16,0},{32,16},{48,32},{64,112},{80,64},{96,80},{112,96},{1... | collective-permute-start | bytes 294920 | tf_op jit(solution)/shard_map/ppermute | solution.py:46
  73.8 4.0 %collective-permute-start.24 = (bf16[32,512]{1,0:T(8,128)(2,1)S(1)}, bf16[32,512]{1,0:T(8,128)(2,1)S(1)}, u32[]{:S(2)}, u32[]{:S(2)}) collective-permute-start(bf16[32,512]{1,0:T(8,128)(2,1)S(1)} %get-tuple-element.86), channel_id=1, source_target_pairs={{0,64},{16,80},{32,96},{48,112},{64,128},{80,144},{96,160},{112,17... | collective-permute-start | bytes 98312 | tf_op jit(solution)/shard_map/ppermute | solution.py:46
  75.1 5.4 %collective-permute-start.25 = (bf16[32,512]{1,0:T(8,128)(2,1)S(1)}, bf16[32,512]{1,0:T(8,128)(2,1)S(1)}, u32[]{:S(2)}, u32[]{:S(2)}) collective-permute-start(bf16[32,512]{1,0:T(8,128)(2,1)S(1)} %get-tuple-element.87), channel_id=1, source_target_pairs={{0,128},{16,144},{32,160},{48,176},{64,192},{80,208},{96,224},{112... | collective-permute-start | bytes 98312 | tf_op jit(solution)/shard_map/ppermute | solution.py:46
  76.9 5.1 %collective-permute-start.26 = (bf16[32,512]{1,0:T(8,128)(2,1)S(1)}, bf16[32,512]{1,0:T(8,128)(2,1)S(1)}, u32[]{:S(2)}, u32[]{:S(2)}) collective-permute-start(bf16[32,512]{1,0:T(8,128)(2,1)S(1)} %get-tuple-element.88), channel_id=1, source_target_pairs={{0,192},{16,208},{32,224},{48,240},{64,0},{80,16},{96,32},{112,48}... | collective-permute-start | bytes 98312 | tf_op jit(solution)/shard_map/ppermute | solution.py:46
  82.1 6.9 %collective-permute-start.27 = (bf16[128,128]{1,0:T(8,128)(2,1)S(1)}, bf16[128,128]{1,0:T(8,128)(2,1)S(1)}, u32[]{:S(2)}, u32[]{:S(2)}) collective-permute-start(bf16[128,128]{1,0:T(8,128)(2,1)S(1)} %get-tuple-element.90), channel_id=1, source_target_pairs={{0,16},{16,32},{32,48},{48,0},{64,80},{80,96},{96,112},{112,64},{1... | collective-permute-start | bytes 98312 | tf_op jit(solution)/shard_map/ppermute | solution.py:46
  84.1 4.9 %collective-permute-start.28 = (bf16[128,128]{1,0:T(8,128)(2,1)S(1)}, bf16[128,128]{1,0:T(8,128)(2,1)S(1)}, u32[]{:S(2)}, u32[]{:S(2)}) collective-permute-start(bf16[128,128]{1,0:T(8,128)(2,1)S(1)} %get-tuple-element.91), channel_id=1, source_target_pairs={{0,32},{16,48},{32,0},{48,16},{64,96},{80,112},{96,64},{112,80},{1... | collective-permute-start | bytes 98312 | tf_op jit(solution)/shard_map/ppermute | solution.py:46
  86.1 4.4 %collective-permute-start.29 = (bf16[128,128]{1,0:T(8,128)(2,1)S(1)}, bf16[128,128]{1,0:T(8,128)(2,1)S(1)}, u32[]{:S(2)}, u32[]{:S(2)}) collective-permute-start(bf16[128,128]{1,0:T(8,128)(2,1)S(1)} %get-tuple-element.92), channel_id=1, source_target_pairs={{0,48},{16,0},{32,16},{48,32},{64,112},{80,64},{96,80},{112,96},{1... | collective-permute-start | bytes 98312 | tf_op jit(solution)/shard_map/ppermute | solution.py:46
  91.1 1.5 %collective-permute-start.30 = (f32[128,384]{1,0:T(8,128)S(1)}, f32[128,384]{1,0:T(8,128)S(1)}, u32[]{:S(2)}, u32[]{:S(2)}) collective-permute-start(f32[128,384]{1,0:T(8,128)S(1)} %get-tuple-element.96), channel_id=1, source_target_pairs={{0,1},{1,0},{2,3},{3,2},{4,5},{5,4},{6,7},{7,6},{8,9},{9,8},{10,11... | collective-permute-start | bytes 589832 | tf_op jit(solution)/shard_map/ppermute | solution.py:30
  92.7 5.4 %collective-permute-start.33 = (f32[32,384]{1,0:T(8,128)S(1)}, f32[32,384]{1,0:T(8,128)S(1)}, u32[]{:S(2)}, u32[]{:S(2)}) collective-permute-start(f32[32,384]{1,0:T(8,128)S(1)} %get-tuple-element.98), channel_id=1, source_target_pairs={{0,6},{1,7},{2,0},{3,1},{4,2},{5,3},{6,4},{7,5},{8,14},{9,15},{10,... | collective-permute-start | bytes 147464 | tf_op jit(solution)/shard_map/ppermute | solution.py:30
  93.6 4.5 %collective-permute-start.32 = (f32[32,384]{1,0:T(8,128)S(1)}, f32[32,384]{1,0:T(8,128)S(1)}, u32[]{:S(2)}, u32[]{:S(2)}) collective-permute-start(f32[32,384]{1,0:T(8,128)S(1)} %get-tuple-element.99), channel_id=1, source_target_pairs={{0,2},{1,3},{2,4},{3,5},{4,6},{5,7},{6,0},{7,1},{8,10},{9,11},{10,... | collective-permute-start | bytes 147464 | tf_op jit(solution)/shard_map/ppermute | solution.py:30
  96.0 5.6 %collective-permute-start.31 = (f32[32,384]{1,0:T(8,128)S(1)}, f32[32,384]{1,0:T(8,128)S(1)}, u32[]{:S(2)}, u32[]{:S(2)}) collective-permute-start(f32[32,384]{1,0:T(8,128)S(1)} %get-tuple-element.100), channel_id=1, source_target_pairs={{0,4},{1,5},{2,6},{3,7},{4,0},{5,1},{6,2},{7,3},{8,12},{9,13},{10,... | collective-permute-start | bytes 147464 | tf_op jit(solution)/shard_map/ppermute | solution.py:30
  101.6 4.9 %copy-start.3 = (bf16[2048,384]{1,0:T(8,128)(2,1)S(1)}, bf16[2048,384]{1,0:T(8,128)(2,1)}, u32[]{:S(2)}) copy-start(bf16[2048,384]{1,0:T(8,128)(2,1)} %dec.1) | copy-start | bytes 4718596
  101.6 7.8 %collective-permute-start.34 = (f32[16,384]{1,0:T(8,128)S(1)}, f32[16,384]{1,0:T(8,128)S(1)}, u32[]{:S(2)}, u32[]{:S(2)}) collective-permute-start(f32[16,384]{1,0:T(8,128)S(1)} %slice_add_fusion.4), channel_id=1, source_target_pairs={{0,8},{1,9},{2,10},{3,11},{4,12},{5,13},{6,14},{7,15},{8,0},{9,1},... | collective-permute-start | bytes 73736 | tf_op jit(solution)/shard_map/ppermute | solution.py:30
  106.5 1.5 %copy-start.2 = (bf16[2048,384]{1,0:T(8,128)(2,1)S(1)}, bf16[2048,384]{1,0:T(8,128)(2,1)}, u32[]{:S(2)}) copy-start(bf16[2048,384]{1,0:T(8,128)(2,1)} %enc.3) | copy-start | bytes 4718596

commit v2 on v1

--- a/solution.py
+++ b/solution.py
@@ -9,7 +9,7 @@
 BF = jnp.bfloat16
 F32 = jnp.float32
 MIB = 1024 * 1024
-FIRST_VMEM = 125 * MIB // 2
+FIRST_VMEM = 60 * MIB
 
 TENSOR_RELS = [(dz, dx, dc) for dz in range(2) for dx in range(4) for dc in range(2)]
 
@@ -272,7 +272,8 @@
 
 
 def context_grad_kernel(*refs):
-    near, far, wenc, out, whole = refs[0], refs[1], refs[2], refs[-2], refs[-1]
+    near, far, wenc, out, flag, whole = refs
+    flag[...] = jnp.zeros_like(flag)
     gather_rows(near, far, whole)
     out[...] = dot(whole[...], wenc[...], ((1,), (1,))).astype(BF)
 
@@ -281,8 +282,8 @@
     return pl.pallas_call(
         context_grad_kernel,
         in_specs=vmem(3),
-        out_specs=vmem(1)[0],
-        out_shape=shape(512, 384),
+        out_specs=vmem(2),
+        out_shape=[shape(512, 384), shape(8, 128, dtype=F32)],
         scratch_shapes=[pltpu.VMEM((512, 2048), BF)],
         compiler_params=params(16),
         cost_estimate=cost(805_000_000, 4 * MIB),
@@ -313,7 +314,8 @@
 
 def second_y_kernel(*refs):
     a_keep, a_got, a_last, b_keep, b_got, b_last = refs[:6]
-    ma_keep, ma_got, mb_keep, mb_got, far, near, a_send, b_send = refs[6:]
+    ma_keep, ma_got, mb_keep, mb_got = refs[6:10]
+    far, near, a_send, b_send = refs[-4:]
     far[...] = add_refs(a_keep[:32, :], a_got[:32, :], a_last[...]).astype(BF)
     near[...] = add_refs(b_keep[:32, :], b_got[:32, :], b_last[...])
     a_send[...] = add_refs(ma_keep[384:, :], ma_got[384:, :]).astype(BF)
@@ -323,7 +325,7 @@
 def second_y(*parts):
     return pl.pallas_call(
         second_y_kernel,
-        in_specs=vmem(10),
+        in_specs=vmem(10) + any_space(len(parts) - 10),
         out_specs=vmem(4),
         out_shape=[shape(32, 2048), shape(32, 2048, dtype=F32)] + [shape(384, 256)] * 2,
         compiler_params=params(8),
@@ -437,11 +439,12 @@
     ma_send, ma_keep, mb_send, mb_keep = moment(packed, packed_far, ctx_t)
     ma_got, mb_got = swap_y(ma_send, 1), swap_y(mb_send, 3)
 
+    context_grad, flag = context_grad_of(packed, packed_far, wenc)
     a_send, b_send = second_x(a_keep, a_got, b_keep, b_got, ma_send)
     a_last, b_last = swap_x(a_send, 3), swap_x(b_send, 1)
 
     far, near, a_send, b_send = second_y(
-        a_keep, a_got, a_last, b_keep, b_got, b_last, ma_keep, ma_got, mb_keep, mb_got
+        a_keep, a_got, a_last, b_keep, b_got, b_last, ma_keep, ma_got, mb_keep, mb_got, flag
     )
     recv = send_tensor(far, (1, 0, 0))
     ma_last, mb_last = swap_y(a_send, 3), swap_y(b_send, 1)
@@ -450,7 +453,6 @@
     code, *codes = code_of(near, recv, subs[1])
     codes = over_z(code_regroup(over_y(codes)))
 
-    context_grad = context_grad_of(packed, packed_far, wenc)
     layer_out = pl.pallas_call(
         layer_out_kernel,
         in_specs=vmem(2),

time: 110 us -> 109 us (level)
  local copies, waits for them, and re-layouts: 4.78 us -> 2.97 us
  waiting for transfers between devices: 42.1 us -> 43.4 us
    ppermute x8, waiting for transfers between devices: 8.39 us -> 11.5 us  [send_tensor(): lax.ppermute(v, 'tensor', [(s, tensor_add(s, rel)) for s in range(16)])]
    ppermute x4, waiting for transfers between devices: 4.88 us -> 2.46 us  [swap_y(): return lax.ppermute(v, 'dp', [(s, s ^ 4 * r) for s in range(16)])]
    ppermute x15, waiting for transfers between devices: 20.6 us -> 22.4 us  [send_dp(): return lax.ppermute(v, 'dp', [(s, dp_add(s, rel)) for s in range(16)])]
    unnamed x18 -> x16, local copies, waits for them, and re-layouts: 4.18 us -> 2.36 us
    ppermute x8, starting transfers between devices: 8.89 us -> 10.1 us  [send_tensor(): lax.ppermute(v, 'tensor', [(s, tensor_add(s, rel)) for s in range(16)])]
    ppermute x4, waiting for transfers between devices: 8.21 us -> 7.08 us  [swap_x(): return lax.ppermute(v, 'tensor', [(s, s ^ 2 * r) for s in range(16)])]
  transfers between devices with their start and end apart: 35 -> 35, of which waited for: 19 -> 20; matrix products, arithmetic and copies ran while one was open for 0% -> 0% of each run, Pallas kernels for 8% -> 8%
where the time goes in v2:
time: 109 us
  starting transfers between devices  48.2 us (44%)
  waiting for transfers between devices  43.4 us (40%)
  Pallas kernels  13.8 us (13%)
  local copies, waits for them, and re-layouts  2.97 us (3%)
    ppermute x15, waiting for transfers between devices, send_dp(): return lax.ppermute(v, 'dp', [(s, dp_add(s, rel)) for s in range(16)])  22.4 us
    ppermute x15, starting transfers between devices, send_dp(): return lax.ppermute(v, 'dp', [(s, dp_add(s, rel)) for s in range(16)])  20.1 us
    ppermute x8, waiting for transfers between devices, send_tensor(): lax.ppermute(v, 'tensor', [(s, tensor_add(s, rel)) for s in range(16)])  11.5 us
    ppermute x4, starting transfers between devices, fetch_tensor(): lax.ppermute(v, 'tensor', [(s, tensor_add(s, rel, -1)) for s in range(16)])  10.1 us
    ppermute x8, starting transfers between devices, send_tensor(): lax.ppermute(v, 'tensor', [(s, tensor_add(s, rel)) for s in range(16)])  10.1 us
    ppermute x4, waiting for transfers between devices, swap_x(): return lax.ppermute(v, 'tensor', [(s, s ^ 2 * r) for s in range(16)])  7.08 us
    ppermute x4, starting transfers between devices, swap_y(): return lax.ppermute(v, 'dp', [(s, s ^ 4 * r) for s in range(16)])  4.54 us
    ppermute x4, starting transfers between devices, swap_x(): return lax.ppermute(v, 'tensor', [(s, s ^ 2 * r) for s in range(16)])  3.38 us
  transfers between devices with their start and end apart: 35, of which 20 were waited for; matrix products, arithmetic and copies ran while one was open for 0% of the time, Pallas kernels for 8%

profile of v2, /device:TPU:30, one launch (start us, length us, event | category | flops | bytes accessed | tf_op | source)
XLA Modules:
  0.0 109.3 jit_solution(12930935874231577088)
XLA Ops:
  0.7 3.0 %grad_code.1 = (bf16[32,2048]{1,0:T(8,128)(2,1)}, bf16[32,1536]{1,0:T(8,128)(2,1)}, bf16[32,1536]{1,0:T(8,128)(2,1)}, bf16[32,1536]{1,0:T(8,128)(2,1)}, bf16[32,1536]{1,0:T(8,128)(2,1)}) custom-call(bf16[32,6144]{1,0:T(8,128)(2,1)} %cot_hbm.1, bf16[2048,384]{1,0:T(8,128)(2,1)} %dec.1), custom_call_target="tpu_custom_call" | custom-call | flops 50000000 | bytes 2097152 | tf_op jit(solution)/shard_map/grad_code/pallas_call | solution.py:412
  3.9 7.2 %collective-permute-start.1 = (bf16[32,2048]{1,0:T(8,128)(2,1)}, bf16[32,2048]{1,0:T(8,128)(2,1)S(1)}, u32[]{:S(2)}, u32[]{:S(2)}) collective-permute-start(bf16[32,2048]{1,0:T(8,128)(2,1)} %get-tuple-element.56.refs_2_), channel_id=1, source_target_pairs={{0,8},{1,9},{2,10},{3,11},{4,12},{5,13},{6,14},{7,15},{8,0},{9,1},... | collective-permute-start | bytes 393224 | tf_op jit(solution)/shard_map/ppermute | solution.py:34
  11.1 2.6 %collective-permute-start.2 = (bf16[32,1536]{1,0:T(8,128)(2,1)}, bf16[32,1536]{1,0:T(8,128)(2,1)S(1)}, u32[]{:S(2)}, u32[]{:S(2)}) collective-permute-start(bf16[32,1536]{1,0:T(8,128)(2,1)} %get-tuple-element.58), channel_id=1, source_target_pairs={{0,128},{16,144},{32,160},{48,176},{64,192},{80,208},{96,224},{112... | collective-permute-start | bytes 294920 | tf_op jit(solution)/shard_map/ppermute | solution.py:46
  13.8 2.3 %copy-done = bf16[384,6144]{1,0:T(8,128)(2,1)S(1)} copy-done((bf16[384,6144]{1,0:T(8,128)(2,1)S(1)}, bf16[384,6144]{1,0:T(8,128)(2,1)}, u32[]{:S(2)}) %copy-start) | copy-done | bytes 4718616
  16.1 2.6 %wenc.1 = (bf16[384,2048]{1,0:T(8,128)(2,1)S(1)}, bf16[384,512]{1,0:T(8,128)(2,1)S(1)}, bf16[512,384]{1,0:T(8,128)(2,1)S(1)}) custom-call(bf16[384,6144]{1,0:T(8,128)(2,1)S(1)} %copy-done, bf16[512,384]{1,0:T(8,128)(2,1)S(1)} %copy-done.3, bf16[2048,384]{1,0:T(8,128)(2,1)S(1)} %copy-done.1, bf16[32,1536]{1,0:T(8,128)(2,1)S(1)} %collective-permute-done.after.refs_5_), custom_call_target="tpu_custom_call" | custom-call | flops 604000000 | bytes 9437184 | tf_op jit(solution)/shard_map/wenc/pallas_call | solution.py:175
  18.7 1.0 collective-permute-done.3.refs_7_
  19.8 1.3 %coded.1 = (bf16[256,2048]{1,0:T(8,128)(2,1)S(1)}, bf16[256,2048]{1,0:T(8,128)(2,1)S(1)}, bf16[64,2048]{1,0:T(8,128)(2,1)S(1)}, bf16[128,384]{1,0:T(8,128)(2,1)S...) custom-call(bf16[512,384]{1,0:T(8,128)(2,1)S(1)} %get-tuple-element.54.refs_0_, ...), custom_call_target="tpu_custom_call" | custom-call | flops 805000000 | bytes 4194304 | tf_op jit(solution)/shard_map/coded/pallas_call | solution.py:201
  21.2 1.1 %collective-permute-start.8 = (bf16[128,384]{1,0:T(8,128)(2,1)S(1)}, bf16[128,384]{1,0:T(8,128)(2,1)S(1)}, u32[]{:S(2)}, u32[]{:S(2)}) collective-permute-start(bf16[128,384]{1,0:T(8,128)(2,1)S(1)} %get-tuple-element.63), channel_id=1, source_target_pairs={{0,16},{16,32},{32,48},{48,0},{64,80},{80,96},{96,112},{112,64},{1... | collective-permute-start | bytes 294920 | tf_op jit(solution)/shard_map/ppermute | solution.py:46
  22.8 2.4 %collective-permute-start.5 = (bf16[64,2048]{1,0:T(8,128)(2,1)S(1)}, bf16[64,2048]{1,0:T(8,128)(2,1)S(1)}, u32[]{:S(2)}, u32[]{:S(2)}) collective-permute-start(bf16[64,2048]{1,0:T(8,128)(2,1)S(1)} %get-tuple-element.60.refs_0_), channel_id=1, source_target_pairs={{0,4},{1,5},{2,6},{3,7},{4,0},{5,1},{6,2},{7,3},{8,12},{9,13},{10,... | collective-permute-start | bytes 786440 | tf_op jit(solution)/shard_map/ppermute | solution.py:34
  25.2 3.0 %collective-permute-done.8.refs_6_.refs_9_ = bf16[128,384]{1,0:T(8,128)(2,1)S(1)} collective-permute-done((bf16[128,384]{1,0:T(8,128)(2,1)S(1)}, bf16[128,384]{1,0:T(8,128)(2,1)S(1)}, u32[]{:S(2)}, u32[]{:S(2)}) %collective-permute-start.8) | collective-permute-done | bytes 98336 | tf_op jit(solution)/shard_map/ppermute | solution.py:46
  28.2 6.3 %collective-permute-done.9.refs_7_.refs_10_ = bf16[128,384]{1,0:T(8,128)(2,1)S(1)} collective-permute-done((bf16[128,384]{1,0:T(8,128)(2,1)S(1)}, bf16[128,384]{1,0:T(8,128)(2,1)S(1)}, u32[]{:S(2)}, u32[]{:S(2)}) %collective-permute-start.9) | collective-permute-done | bytes 98336 | tf_op jit(solution)/shard_map/ppermute | solution.py:46
  34.5 1.2 %collective-permute-start.10 = (bf16[128,384]{1,0:T(8,128)(2,1)S(1)}, bf16[128,384]{1,0:T(8,128)(2,1)S(1)}, u32[]{:S(2)}, u32[]{:S(2)}) collective-permute-start(bf16[128,384]{1,0:T(8,128)(2,1)S(1)} %get-tuple-element.65), channel_id=1, source_target_pairs={{0,48},{16,0},{32,16},{48,32},{64,112},{80,64},{96,80},{112,96},{1... | collective-permute-start | bytes 294920 | tf_op jit(solution)/shard_map/ppermute | solution.py:46
  35.7 3.4 %collective-permute-done.10.refs_8_.refs_11_ = bf16[128,384]{1,0:T(8,128)(2,1)S(1)} collective-permute-done((bf16[128,384]{1,0:T(8,128)(2,1)S(1)}, bf16[128,384]{1,0:T(8,128)(2,1)S(1)}, u32[]{:S(2)}, u32[]{:S(2)}) %collective-permute-start.10) | collective-permute-done | bytes 98336 | tf_op jit(solution)/shard_map/ppermute | solution.py:46
  39.5 0.9 collective-permute-start.11
  40.5 1.2 %collective-permute-start.12 = (bf16[64,2048]{1,0:T(8,128)(2,1)S(1)}, bf16[64,2048]{1,0:T(8,128)(2,1)S(1)}, u32[]{:S(2)}, u32[]{:S(2)}) collective-permute-start(bf16[64,2048]{1,0:T(8,128)(2,1)S(1)} %get-tuple-element.69), channel_id=1, source_target_pairs={{0,6},{1,7},{2,4},{3,5},{4,2},{5,3},{6,0},{7,1},{8,14},{9,15},{10,... | collective-permute-start | bytes 786440 | tf_op jit(solution)/shard_map/ppermute | solution.py:38
  41.6 0.5 collective-permute-done.13.far.refs_1_
  42.2 1.2 %moment.1 = (bf16[768,256]{1,0:T(8,128)(2,1)S(1)}, bf16[768,256]{1,0:T(8,128)(2,1)S(1)}, bf16[768,256]{1,0:T(8,128)(2,1)S(1)}, bf16[768,256]{1,0:T(8,128)(2,1)S(1)}) custom-call(bf16[256,2048]{1,0:T(8,128)(2,1)S(1)} %get-tuple-element.70.near.refs_0_, bf16[256,2048]{1,0:T(8,128)(2,1)S(1)} %collective-permute-done.13.far.refs_1_, ...), custom_call_target="tpu_custom_call" | custom-call | flops 805000000 | bytes 4194304 | tf_op jit(solution)/shard_map/moment/pallas_call | solution.py:262
  43.4 2.3 %collective-permute-start.17 = (bf16[768,256]{1,0:T(8,128)(2,1)S(1)}, bf16[768,256]{1,0:T(8,128)(2,1)S(1)}, u32[]{:S(2)}, u32[]{:S(2)}) collective-permute-start(bf16[768,256]{1,0:T(8,128)(2,1)S(1)} %get-tuple-element.77), channel_id=1, source_target_pairs={{0,192},{16,208},{32,224},{48,240},{64,128},{80,144},{96,160},{112... | collective-permute-start | bytes 1179656 | tf_op jit(solution)/shard_map/ppermute | solution.py:42
  45.8 2.5 %collective-permute-done.11.a_got.refs_1_ = bf16[64,2048]{1,0:T(8,128)(2,1)S(1)} collective-permute-done((bf16[64,2048]{1,0:T(8,128)(2,1)S(1)}, bf16[64,2048]{1,0:T(8,128)(2,1)S(1)}, u32[]{:S(2)}, u32[]{:S(2)}) %collective-permute-start.11) | collective-permute-done | bytes 262176 | tf_op jit(solution)/shard_map/ppermute | solution.py:38
  48.3 1.8 %collective-permute-done.12.b_got.refs_4_ = bf16[64,2048]{1,0:T(8,128)(2,1)S(1)} collective-permute-done((bf16[64,2048]{1,0:T(8,128)(2,1)S(1)}, bf16[64,2048]{1,0:T(8,128)(2,1)S(1)}, u32[]{:S(2)}, u32[]{:S(2)}) %collective-permute-start.12) | collective-permute-done | bytes 262176 | tf_op jit(solution)/shard_map/ppermute | solution.py:38
  50.1 1.3 %collective-permute-start.14 = (bf16[32,2048]{1,0:T(8,128)(2,1)S(1)}, bf16[32,2048]{1,0:T(8,128)(2,1)S(1)}, u32[]{:S(2)}, u32[]{:S(2)}) collective-permute-start(bf16[32,2048]{1,0:T(8,128)(2,1)S(1)} %get-tuple-element.73), channel_id=1, source_target_pairs={{0,6},{1,7},{2,4},{3,5},{4,2},{5,3},{6,0},{7,1},{8,14},{9,15},{10,... | collective-permute-start | bytes 393224 | tf_op jit(solution)/shard_map/ppermute | solution.py:38
  51.4 2.1 %context_grad.1 = (bf16[512,384]{1,0:T(8,128)(2,1)}, f32[8,128]{1,0:T(8,128)S(1)}) custom-call(bf16[256,2048]{1,0:T(8,128)(2,1)S(1)} %get-tuple-element.70.near.refs_0_, bf16[256,2048]{1,0:T(8,128)(2,1)S(1)} %collective-permute-done.13.far.refs_1_, bf16[384,2048]{1,0:T(8,128)(2,1)S(1)} %get-tuple-element.55.refs_1_.refs_2_), custom_call_target="tpu_custom_call" | custom-call | flops 805000000 | bytes 4194304 | tf_op jit(solution)/shard_map/context_grad/pallas_call | solution.py:282
  53.5 2.8 %collective-permute-done.14.refs_2_ = bf16[32,2048]{1,0:T(8,128)(2,1)S(1)} collective-permute-done((bf16[32,2048]{1,0:T(8,128)(2,1)S(1)}, bf16[32,2048]{1,0:T(8,128)(2,1)S(1)}, u32[]{:S(2)}, u32[]{:S(2)}) %collective-permute-start.14) | collective-permute-done | bytes 131104 | tf_op jit(solution)/shard_map/ppermute | solution.py:38
  56.8 2.1 %collective-permute-start.19 = (bf16[384,256]{1,0:T(8,128)(2,1)S(1)}, bf16[384,256]{1,0:T(8,128)(2,1)S(1)}, u32[]{:S(2)}, u32[]{:S(2)}) collective-permute-start(bf16[384,256]{1,0:T(8,128)(2,1)S(1)} %get-tuple-element.81), channel_id=1, source_target_pairs={{0,192},{16,208},{32,224},{48,240},{64,128},{80,144},{96,160},{112... | collective-permute-start | bytes 589832 | tf_op jit(solution)/shard_map/ppermute | solution.py:42
  58.9 3.4 %collective-permute-start.18 = (bf16[32,2048]{1,0:T(8,128)(2,1)S(1)}, bf16[32,2048]{1,0:T(8,128)(2,1)S(1)}, u32[]{:S(2)}, u32[]{:S(2)}) collective-permute-start(bf16[32,2048]{1,0:T(8,128)(2,1)S(1)} %get-tuple-element.80), channel_id=1, source_target_pairs={{0,8},{1,9},{2,10},{3,11},{4,12},{5,13},{6,14},{7,15},{8,0},{9,1},... | collective-permute-start | bytes 393224 | tf_op jit(solution)/shard_map/ppermute | solution.py:30
  62.3 1.5 %collective-permute-done.19.a_last = bf16[384,256]{1,0:T(8,128)(2,1)S(1)} collective-permute-done((bf16[384,256]{1,0:T(8,128)(2,1)S(1)}, bf16[384,256]{1,0:T(8,128)(2,1)S(1)}, u32[]{:S(2)}, u32[]{:S(2)}) %collective-permute-start.19) | collective-permute-done | bytes 196640 | tf_op jit(solution)/shard_map/ppermute | solution.py:42
  63.9 0.7 collective-permute-done.20.b_last
  64.9 4.4 %collective-permute-start.22 = (bf16[384,128]{1,0:T(8,128)(2,1)S(1)}, bf16[384,128]{1,0:T(8,128)(2,1)S(1)}, u32[]{:S(2)}, u32[]{:S(2)}) collective-permute-start(bf16[384,128]{1,0:T(8,128)(2,1)S(1)} %get-tuple-element.87), channel_id=1, source_target_pairs={{0,32},{16,48},{32,0},{48,16},{64,96},{80,112},{96,64},{112,80},{1... | collective-permute-start | bytes 294920 | tf_op jit(solution)/shard_map/ppermute | solution.py:46
  69.3 1.4 %collective-permute-done.18.recv = bf16[32,2048]{1,0:T(8,128)(2,1)S(1)} collective-permute-done((bf16[32,2048]{1,0:T(8,128)(2,1)S(1)}, bf16[32,2048]{1,0:T(8,128)(2,1)S(1)}, u32[]{:S(2)}, u32[]{:S(2)}) %collective-permute-start.18) | collective-permute-done | bytes 131104 | tf_op jit(solution)/shard_map/ppermute | solution.py:30
  70.7 2.0 %collective-permute-done.21.after.refs_1_ = bf16[384,128]{1,0:T(8,128)(2,1)S(1)} collective-permute-done((bf16[384,128]{1,0:T(8,128)(2,1)S(1)}, bf16[384,128]{1,0:T(8,128)(2,1)S(1)}, u32[]{:S(2)}, u32[]{:S(2)}) %collective-permute-start.21) | collective-permute-done | bytes 98336 | tf_op jit(solution)/shard_map/ppermute | solution.py:46
  72.7 1.6 %collective-permute-start.24 = (bf16[32,512]{1,0:T(8,128)(2,1)S(1)}, bf16[32,512]{1,0:T(8,128)(2,1)S(1)}, u32[]{:S(2)}, u32[]{:S(2)}) collective-permute-start(bf16[32,512]{1,0:T(8,128)(2,1)S(1)} %get-tuple-element.90), channel_id=1, source_target_pairs={{0,64},{16,80},{32,96},{48,112},{64,128},{80,144},{96,160},{112,17... | collective-permute-start | bytes 98312 | tf_op jit(solution)/shard_map/ppermute | solution.py:46
  74.3 2.5 %collective-permute-start.25 = (bf16[32,512]{1,0:T(8,128)(2,1)S(1)}, bf16[32,512]{1,0:T(8,128)(2,1)S(1)}, u32[]{:S(2)}, u32[]{:S(2)}) collective-permute-start(bf16[32,512]{1,0:T(8,128)(2,1)S(1)} %get-tuple-element.91), channel_id=1, source_target_pairs={{0,128},{16,144},{32,160},{48,176},{64,192},{80,208},{96,224},{112... | collective-permute-start | bytes 98312 | tf_op jit(solution)/shard_map/ppermute | solution.py:46
  76.8 2.9 %collective-permute-done.25.refs_2_ = bf16[32,512]{1,0:T(8,128)(2,1)S(1)} collective-permute-done((bf16[32,512]{1,0:T(8,128)(2,1)S(1)}, bf16[32,512]{1,0:T(8,128)(2,1)S(1)}, u32[]{:S(2)}, u32[]{:S(2)}) %collective-permute-start.25) | collective-permute-done | bytes 32800 | tf_op jit(solution)/shard_map/ppermute | solution.py:46
  79.8 2.2 %collective-permute-done.26.refs_3_ = bf16[32,512]{1,0:T(8,128)(2,1)S(1)} collective-permute-done((bf16[32,512]{1,0:T(8,128)(2,1)S(1)}, bf16[32,512]{1,0:T(8,128)(2,1)S(1)}, u32[]{:S(2)}, u32[]{:S(2)}) %collective-permute-start.26) | collective-permute-done | bytes 32800 | tf_op jit(solution)/shard_map/ppermute | solution.py:46
  82.0 1.3 %collective-permute-start.27 = (bf16[128,128]{1,0:T(8,128)(2,1)S(1)}, bf16[128,128]{1,0:T(8,128)(2,1)S(1)}, u32[]{:S(2)}, u32[]{:S(2)}) collective-permute-start(bf16[128,128]{1,0:T(8,128)(2,1)S(1)} %get-tuple-element.94), channel_id=1, source_target_pairs={{0,16},{16,32},{32,48},{48,0},{64,80},{80,96},{96,112},{112,64},{1... | collective-permute-start | bytes 98312 | tf_op jit(solution)/shard_map/ppermute | solution.py:46
  83.3 2.0 %collective-permute-start.28 = (bf16[128,128]{1,0:T(8,128)(2,1)S(1)}, bf16[128,128]{1,0:T(8,128)(2,1)S(1)}, u32[]{:S(2)}, u32[]{:S(2)}) collective-permute-start(bf16[128,128]{1,0:T(8,128)(2,1)S(1)} %get-tuple-element.95), channel_id=1, source_target_pairs={{0,32},{16,48},{32,0},{48,16},{64,96},{80,112},{96,64},{112,80},{1... | collective-permute-start | bytes 98312 | tf_op jit(solution)/shard_map/ppermute | solution.py:46
  85.3 2.8 %collective-permute-start.29 = (bf16[128,128]{1,0:T(8,128)(2,1)S(1)}, bf16[128,128]{1,0:T(8,128)(2,1)S(1)}, u32[]{:S(2)}, u32[]{:S(2)}) collective-permute-start(bf16[128,128]{1,0:T(8,128)(2,1)S(1)} %get-tuple-element.96), channel_id=1, source_target_pairs={{0,48},{16,0},{32,16},{48,32},{64,112},{80,64},{96,80},{112,96},{1... | collective-permute-start | bytes 98312 | tf_op jit(solution)/shard_map/ppermute | solution.py:46
  88.2 1.6 %collective-permute-done.29.refs_7_ = bf16[128,128]{1,0:T(8,128)(2,1)S(1)} collective-permute-done((bf16[128,128]{1,0:T(8,128)(2,1)S(1)}, bf16[128,128]{1,0:T(8,128)(2,1)S(1)}, u32[]{:S(2)}, u32[]{:S(2)}) %collective-permute-start.29) | collective-permute-done | bytes 32800 | tf_op jit(solution)/shard_map/ppermute | solution.py:46
  89.8 0.6 codec_grads.1
  90.4 1.4 %collective-permute-done.30 = f32[128,384]{1,0:T(8,128)S(1)} collective-permute-done((f32[128,384]{1,0:T(8,128)S(1)}, f32[128,384]{1,0:T(8,128)S(1)}, u32[]{:S(2)}, u32[]{:S(2)}) %collective-permute-start.30) | collective-permute-done | bytes 196640 | tf_op jit(solution)/shard_map/ppermute | solution.py:30
  92.3 2.9 %collective-permute-start.32 = (f32[32,384]{1,0:T(8,128)S(1)}, f32[32,384]{1,0:T(8,128)S(1)}, u32[]{:S(2)}, u32[]{:S(2)}) collective-permute-start(f32[32,384]{1,0:T(8,128)S(1)} %get-tuple-element.103), channel_id=1, source_target_pairs={{0,2},{1,3},{2,4},{3,5},{4,6},{5,7},{6,0},{7,1},{8,10},{9,11},{10,... | collective-permute-start | bytes 147464 | tf_op jit(solution)/shard_map/ppermute | solution.py:30
  95.4 1.9 %collective-permute-done.33 = f32[32,384]{1,0:T(8,128)S(1)} collective-permute-done((f32[32,384]{1,0:T(8,128)S(1)}, f32[32,384]{1,0:T(8,128)S(1)}, u32[]{:S(2)}, u32[]{:S(2)}) %collective-permute-start.33) | collective-permute-done | bytes 49184 | tf_op jit(solution)/shard_map/ppermute | solution.py:30
  97.3 3.5 %collective-permute-done.31 = f32[32,384]{1,0:T(8,128)S(1)} collective-permute-done((f32[32,384]{1,0:T(8,128)S(1)}, f32[32,384]{1,0:T(8,128)S(1)}, u32[]{:S(2)}, u32[]{:S(2)}) %collective-permute-start.31) | collective-permute-done | bytes 49184 | tf_op jit(solution)/shard_map/ppermute | solution.py:30
  100.8 2.9 %collective-permute-start.34 = (f32[16,384]{1,0:T(8,128)S(1)}, f32[16,384]{1,0:T(8,128)S(1)}, u32[]{:S(2)}, u32[]{:S(2)}) collective-permute-start(f32[16,384]{1,0:T(8,128)S(1)} %slice_add_fusion.4), channel_id=1, source_target_pairs={{0,8},{1,9},{2,10},{3,11},{4,12},{5,13},{6,14},{7,15},{8,0},{9,1},... | collective-permute-start | bytes 73736 | tf_op jit(solution)/shard_map/ppermute | solution.py:30
  103.8 1.1 %layer_out.1 = bf16[32,6144]{1,0:T(8,128)(2,1)} custom-call(bf16[32,2048]{1,0:T(8,128)(2,1)S(1)} %get-tuple-element.84.code, bf16[2048,384]{1,0:T(8,128)(2,1)S(1)} %copy-done.2), custom_call_target="tpu_custom_call" | custom-call | flops 50000000 | bytes 2097152 | tf_op jit(solution)/shard_map/layer_out/pallas_call | solution.py:456
  104.9 1.0 w_out_grad.1
  105.9 2.7 %collective-permute-done.34 = f32[16,384]{1,0:T(8,128)S(1)} collective-permute-done((f32[16,384]{1,0:T(8,128)S(1)}, f32[16,384]{1,0:T(8,128)S(1)}, u32[]{:S(2)}, u32[]{:S(2)}) %collective-permute-start.34) | collective-permute-done | bytes 24608 | tf_op jit(solution)/shard_map/ppermute | solution.py:30
  108.7 0.6 fusion.1
  (57 shorter events, 3.2 us)
Async XLA Ops:
  0.6 13.1 %copy-start.1 = (bf16[2048,384]{1,0:T(8,128)(2,1)S(1)}, bf16[2048,384]{1,0:T(8,128)(2,1)}, u32[]{:S(2)}) copy-start(bf16[2048,384]{1,0:T(8,128)(2,1)} %enc.3) | copy-start | bytes 4718596
  0.6 13.1 %copy-start.3 = (bf16[512,384]{1,0:T(8,128)(2,1)S(1)}, bf16[512,384]{1,0:T(8,128)(2,1)}, u32[]{:S(2)}) copy-start(bf16[512,384]{1,0:T(8,128)(2,1)} %ctx.1) | copy-start | bytes 1179652
  3.6 10.1 %collective-permute-start = (bf16[32,1536]{1,0:T(8,128)(2,1)}, bf16[32,1536]{1,0:T(8,128)(2,1)S(1)}, u32[]{:S(2)}, u32[]{:S(2)}) collective-permute-start(bf16[32,1536]{1,0:T(8,128)(2,1)} %get-tuple-element.53), channel_id=1, source_target_pairs={{0,64},{16,80},{32,96},{48,112},{64,128},{80,144},{96,160},{112,17... | collective-permute-start | bytes 294920 | tf_op jit(solution)/shard_map/ppermute | solution.py:46
  3.9 15.8 %collective-permute-start.1 = (bf16[32,2048]{1,0:T(8,128)(2,1)}, bf16[32,2048]{1,0:T(8,128)(2,1)S(1)}, u32[]{:S(2)}, u32[]{:S(2)}) collective-permute-start(bf16[32,2048]{1,0:T(8,128)(2,1)} %get-tuple-element.56.refs_2_), channel_id=1, source_target_pairs={{0,8},{1,9},{2,10},{3,11},{4,12},{5,13},{6,14},{7,15},{8,0},{9,1},... | collective-permute-start | bytes 393224 | tf_op jit(solution)/shard_map/ppermute | solution.py:34
  11.1 7.6 %collective-permute-start.2 = (bf16[32,1536]{1,0:T(8,128)(2,1)}, bf16[32,1536]{1,0:T(8,128)(2,1)S(1)}, u32[]{:S(2)}, u32[]{:S(2)}) collective-permute-start(bf16[32,1536]{1,0:T(8,128)(2,1)} %get-tuple-element.58), channel_id=1, source_target_pairs={{0,128},{16,144},{32,160},{48,176},{64,192},{80,208},{96,224},{112... | collective-permute-start | bytes 294920 | tf_op jit(solution)/shard_map/ppermute | solution.py:46
  13.7 6.0 %collective-permute-start.3 = (bf16[32,1536]{1,0:T(8,128)(2,1)}, bf16[32,1536]{1,0:T(8,128)(2,1)S(1)}, u32[]{:S(2)}, u32[]{:S(2)}) collective-permute-start(bf16[32,1536]{1,0:T(8,128)(2,1)} %get-tuple-element.59), channel_id=1, source_target_pairs={{0,192},{16,208},{32,224},{48,240},{64,0},{80,16},{96,32},{112,48}... | collective-permute-start | bytes 294920 | tf_op jit(solution)/shard_map/ppermute | solution.py:46
  13.7 2.3 %copy-start = (bf16[384,6144]{1,0:T(8,128)(2,1)S(1)}, bf16[384,6144]{1,0:T(8,128)(2,1)}, u32[]{:S(2)}) copy-start(bf16[384,6144]{1,0:T(8,128)(2,1)} %w_hbm.3) | copy-start | bytes 14155780
  16.1 3.7 %copy-start.4 = (bf16[32,2048]{1,0:T(8,128)(2,1)S(1)}, bf16[32,2048]{1,0:T(8,128)(2,1)}, u32[]{:S(2)}) copy-start(bf16[32,2048]{1,0:T(8,128)(2,1)} %get-tuple-element.56.refs_2_) | copy-start | bytes 393220
  16.1 3.7 %copy-start.5 = (bf16[32,1536]{1,0:T(8,128)(2,1)S(1)}, bf16[32,1536]{1,0:T(8,128)(2,1)}, u32[]{:S(2)}) copy-start(bf16[32,1536]{1,0:T(8,128)(2,1)} %get-tuple-element.57.refs_4_) | copy-start | bytes 294916
  21.1 18.0 %collective-permute-start.7 = (bf16[256,2048]{1,0:T(8,128)(2,1)S(1)}, bf16[256,2048]{1,0:T(8,128)(2,1)S(1)}, u32[]{:S(2)}, u32[]{:S(2)}) collective-permute-start(bf16[256,2048]{1,0:T(8,128)(2,1)S(1)} %get-tuple-element.62), channel_id=1, source_target_pairs={{0,1},{1,0},{2,3},{3,2},{4,5},{5,4},{6,7},{7,6},{8,9},{9,8},{10,11... | collective-permute-start | bytes 3145736 | tf_op jit(solution)/shard_map/ppermute | solution.py:30
  21.2 7.0 %collective-permute-start.8 = (bf16[128,384]{1,0:T(8,128)(2,1)S(1)}, bf16[128,384]{1,0:T(8,128)(2,1)S(1)}, u32[]{:S(2)}, u32[]{:S(2)}) collective-permute-start(bf16[128,384]{1,0:T(8,128)(2,1)S(1)} %get-tuple-element.63), channel_id=1, source_target_pairs={{0,16},{16,32},{32,48},{48,0},{64,80},{80,96},{96,112},{112,64},{1... | collective-permute-start | bytes 294920 | tf_op jit(solution)/shard_map/ppermute | solution.py:46
  22.3 16.8 %collective-permute-start.6 = (bf16[64,2048]{1,0:T(8,128)(2,1)S(1)}, bf16[64,2048]{1,0:T(8,128)(2,1)S(1)}, u32[]{:S(2)}, u32[]{:S(2)}) collective-permute-start(bf16[64,2048]{1,0:T(8,128)(2,1)S(1)} %get-tuple-element.60.refs_0_), channel_id=1, source_target_pairs={{0,2},{1,3},{2,4},{3,5},{4,6},{5,7},{6,0},{7,1},{8,10},{9,11},{10,... | collective-permute-start | bytes 786440 | tf_op jit(solution)/shard_map/ppermute | solution.py:34
  22.8 16.3 %collective-permute-start.5 = (bf16[64,2048]{1,0:T(8,128)(2,1)S(1)}, bf16[64,2048]{1,0:T(8,128)(2,1)S(1)}, u32[]{:S(2)}, u32[]{:S(2)}) collective-permute-start(bf16[64,2048]{1,0:T(8,128)(2,1)S(1)} %get-tuple-element.60.refs_0_), channel_id=1, source_target_pairs={{0,4},{1,5},{2,6},{3,7},{4,0},{5,1},{6,2},{7,3},{8,12},{9,13},{10,... | collective-permute-start | bytes 786440 | tf_op jit(solution)/shard_map/ppermute | solution.py:34
  25.2 13.9 %collective-permute-start.4 = (bf16[64,2048]{1,0:T(8,128)(2,1)S(1)}, bf16[64,2048]{1,0:T(8,128)(2,1)S(1)}, u32[]{:S(2)}, u32[]{:S(2)}) collective-permute-start(bf16[64,2048]{1,0:T(8,128)(2,1)S(1)} %get-tuple-element.60.refs_0_), channel_id=1, source_target_pairs={{0,6},{1,7},{2,0},{3,1},{4,2},{5,3},{6,4},{7,5},{8,14},{9,15},{10,... | collective-permute-start | bytes 786440 | tf_op jit(solution)/shard_map/ppermute | solution.py:34
  28.2 6.3 %collective-permute-start.9 = (bf16[128,384]{1,0:T(8,128)(2,1)S(1)}, bf16[128,384]{1,0:T(8,128)(2,1)S(1)}, u32[]{:S(2)}, u32[]{:S(2)}) collective-permute-start(bf16[128,384]{1,0:T(8,128)(2,1)S(1)} %get-tuple-element.64), channel_id=1, source_target_pairs={{0,32},{16,48},{32,0},{48,16},{64,96},{80,112},{96,64},{112,80},{1... | collective-permute-start | bytes 294920 | tf_op jit(solution)/shard_map/ppermute | solution.py:46
  34.5 4.6 %collective-permute-start.10 = (bf16[128,384]{1,0:T(8,128)(2,1)S(1)}, bf16[128,384]{1,0:T(8,128)(2,1)S(1)}, u32[]{:S(2)}, u32[]{:S(2)}) collective-permute-start(bf16[128,384]{1,0:T(8,128)(2,1)S(1)} %get-tuple-element.65), channel_id=1, source_target_pairs={{0,48},{16,0},{32,16},{48,32},{64,112},{80,64},{96,80},{112,96},{1... | collective-permute-start | bytes 294920 | tf_op jit(solution)/shard_map/ppermute | solution.py:46
  39.4 2.7 %collective-permute-start.13 = (bf16[256,2048]{1,0:T(8,128)(2,1)S(1)}, bf16[256,2048]{1,0:T(8,128)(2,1)S(1)}, u32[]{:S(2)}, u32[]{:S(2)}) collective-permute-start(bf16[256,2048]{1,0:T(8,128)(2,1)S(1)} %get-tuple-element.70.near.refs_0_), channel_id=1, source_target_pairs={{0,1},{1,0},{2,3},{3,2},{4,5},{5,4},{6,7},{7,6},{8,9},{9,8},{10,11... | collective-permute-start | bytes 3145736 | tf_op jit(solution)/shard_map/ppermute | solution.py:30
  39.5 8.7 %collective-permute-start.11 = (bf16[64,2048]{1,0:T(8,128)(2,1)S(1)}, bf16[64,2048]{1,0:T(8,128)(2,1)S(1)}, u32[]{:S(2)}, u32[]{:S(2)}) collective-permute-start(bf16[64,2048]{1,0:T(8,128)(2,1)S(1)} %get-tuple-element.67), channel_id=1, source_target_pairs={{0,2},{1,3},{2,0},{3,1},{4,6},{5,7},{6,4},{7,5},{8,10},{9,11},{10,... | collective-permute-start | bytes 786440 | tf_op jit(solution)/shard_map/ppermute | solution.py:38
  40.5 9.6 %collective-permute-start.12 = (bf16[64,2048]{1,0:T(8,128)(2,1)S(1)}, bf16[64,2048]{1,0:T(8,128)(2,1)S(1)}, u32[]{:S(2)}, u32[]{:S(2)}) collective-permute-start(bf16[64,2048]{1,0:T(8,128)(2,1)S(1)} %get-tuple-element.69), channel_id=1, source_target_pairs={{0,6},{1,7},{2,4},{3,5},{4,2},{5,3},{6,0},{7,1},{8,14},{9,15},{10,... | collective-permute-start | bytes 786440 | tf_op jit(solution)/shard_map/ppermute | solution.py:38
  42.2 47.6 %slice-start = ((s8[4718592]{0:T(1024)(128)(4,1)}), s8[524288]{0:T(1024)(128)(4,1)S(1)}, s32[]{:S(2)}) async-start(s8[4718592]{0:T(1024)(128)(4,1)} %bitcast), calls=%async_computation | async-start | bytes 1048576
  43.4 12.9 %collective-permute-start.17 = (bf16[768,256]{1,0:T(8,128)(2,1)S(1)}, bf16[768,256]{1,0:T(8,128)(2,1)S(1)}, u32[]{:S(2)}, u32[]{:S(2)}) collective-permute-start(bf16[768,256]{1,0:T(8,128)(2,1)S(1)} %get-tuple-element.77), channel_id=1, source_target_pairs={{0,192},{16,208},{32,224},{48,240},{64,128},{80,144},{96,160},{112... | collective-permute-start | bytes 1179656 | tf_op jit(solution)/shard_map/ppermute | solution.py:42
  45.7 10.9 %collective-permute-start.16 = (bf16[768,256]{1,0:T(8,128)(2,1)S(1)}, bf16[768,256]{1,0:T(8,128)(2,1)S(1)}, u32[]{:S(2)}, u32[]{:S(2)}) collective-permute-start(bf16[768,256]{1,0:T(8,128)(2,1)S(1)} %get-tuple-element.72.after), channel_id=1, source_target_pairs={{0,64},{16,80},{32,96},{48,112},{64,0},{80,16},{96,32},{112,48},{1... | collective-permute-start | bytes 1179656 | tf_op jit(solution)/shard_map/ppermute | solution.py:42
  50.1 6.3 %collective-permute-start.14 = (bf16[32,2048]{1,0:T(8,128)(2,1)S(1)}, bf16[32,2048]{1,0:T(8,128)(2,1)S(1)}, u32[]{:S(2)}, u32[]{:S(2)}) collective-permute-start(bf16[32,2048]{1,0:T(8,128)(2,1)S(1)} %get-tuple-element.73), channel_id=1, source_target_pairs={{0,6},{1,7},{2,4},{3,5},{4,2},{5,3},{6,0},{7,1},{8,14},{9,15},{10,... | collective-permute-start | bytes 393224 | tf_op jit(solution)/shard_map/ppermute | solution.py:38
  51.4 38.4 %slice-start.1 = ((s8[4718592]{0:T(1024)(128)(4,1)}), s8[4194304]{0:T(1024)(128)(4,1)S(1)}, s32[]{:S(2)}) async-start(s8[4718592]{0:T(1024)(128)(4,1)} %bitcast), calls=%async_computation.1 | async-start | bytes 8388608
  51.4 5.0 %collective-permute-start.15 = (bf16[32,2048]{1,0:T(8,128)(2,1)S(1)}, bf16[32,2048]{1,0:T(8,128)(2,1)S(1)}, u32[]{:S(2)}, u32[]{:S(2)}) collective-permute-start(bf16[32,2048]{1,0:T(8,128)(2,1)S(1)} %get-tuple-element.74), channel_id=1, source_target_pairs={{0,2},{1,3},{2,0},{3,1},{4,6},{5,7},{6,4},{7,5},{8,10},{9,11},{10,... | collective-permute-start | bytes 393224 | tf_op jit(solution)/shard_map/ppermute | solution.py:38
  56.8 7.1 %collective-permute-start.19 = (bf16[384,256]{1,0:T(8,128)(2,1)S(1)}, bf16[384,256]{1,0:T(8,128)(2,1)S(1)}, u32[]{:S(2)}, u32[]{:S(2)}) collective-permute-start(bf16[384,256]{1,0:T(8,128)(2,1)S(1)} %get-tuple-element.81), channel_id=1, source_target_pairs={{0,192},{16,208},{32,224},{48,240},{64,128},{80,144},{96,160},{112... | collective-permute-start | bytes 589832 | tf_op jit(solution)/shard_map/ppermute | solution.py:42
  58.9 5.7 %collective-permute-start.20 = (bf16[384,256]{1,0:T(8,128)(2,1)S(1)}, bf16[384,256]{1,0:T(8,128)(2,1)S(1)}, u32[]{:S(2)}, u32[]{:S(2)}) collective-permute-start(bf16[384,256]{1,0:T(8,128)(2,1)S(1)} %get-tuple-element.82), channel_id=1, source_target_pairs={{0,64},{16,80},{32,96},{48,112},{64,0},{80,16},{96,32},{112,48},{1... | collective-permute-start | bytes 589832 | tf_op jit(solution)/shard_map/ppermute | solution.py:42
  58.9 11.8 %collective-permute-start.18 = (bf16[32,2048]{1,0:T(8,128)(2,1)S(1)}, bf16[32,2048]{1,0:T(8,128)(2,1)S(1)}, u32[]{:S(2)}, u32[]{:S(2)}) collective-permute-start(bf16[32,2048]{1,0:T(8,128)(2,1)S(1)} %get-tuple-element.80), channel_id=1, source_target_pairs={{0,8},{1,9},{2,10},{3,11},{4,12},{5,13},{6,14},{7,15},{8,0},{9,1},... | collective-permute-start | bytes 393224 | tf_op jit(solution)/shard_map/ppermute | solution.py:30
  64.7 8.0 %collective-permute-start.21 = (bf16[384,128]{1,0:T(8,128)(2,1)S(1)}, bf16[384,128]{1,0:T(8,128)(2,1)S(1)}, u32[]{:S(2)}, u32[]{:S(2)}) collective-permute-start(bf16[384,128]{1,0:T(8,128)(2,1)S(1)} %get-tuple-element.83), channel_id=1, source_target_pairs={{0,16},{16,32},{32,48},{48,0},{64,80},{80,96},{96,112},{112,64},{1... | collective-permute-start | bytes 294920 | tf_op jit(solution)/shard_map/ppermute | solution.py:46
  64.9 23.3 %collective-permute-start.22 = (bf16[384,128]{1,0:T(8,128)(2,1)S(1)}, bf16[384,128]{1,0:T(8,128)(2,1)S(1)}, u32[]{:S(2)}, u32[]{:S(2)}) collective-permute-start(bf16[384,128]{1,0:T(8,128)(2,1)S(1)} %get-tuple-element.87), channel_id=1, source_target_pairs={{0,32},{16,48},{32,0},{48,16},{64,96},{80,112},{96,64},{112,80},{1... | collective-permute-start | bytes 294920 | tf_op jit(solution)/shard_map/ppermute | solution.py:46
  69.3 18.9 %collective-permute-start.23 = (bf16[384,128]{1,0:T(8,128)(2,1)S(1)}, bf16[384,128]{1,0:T(8,128)(2,1)S(1)}, u32[]{:S(2)}, u32[]{:S(2)}) collective-permute-start(bf16[384,128]{1,0:T(8,128)(2,1)S(1)} %get-tuple-element.88), channel_id=1, source_target_pairs={{0,48},{16,0},{32,16},{48,32},{64,112},{80,64},{96,80},{112,96},{1... | collective-permute-start | bytes 294920 | tf_op jit(solution)/shard_map/ppermute | solution.py:46
  72.7 4.1 %collective-permute-start.24 = (bf16[32,512]{1,0:T(8,128)(2,1)S(1)}, bf16[32,512]{1,0:T(8,128)(2,1)S(1)}, u32[]{:S(2)}, u32[]{:S(2)}) collective-permute-start(bf16[32,512]{1,0:T(8,128)(2,1)S(1)} %get-tuple-element.90), channel_id=1, source_target_pairs={{0,64},{16,80},{32,96},{48,112},{64,128},{80,144},{96,160},{112,17... | collective-permute-start | bytes 98312 | tf_op jit(solution)/shard_map/ppermute | solution.py:46
  74.3 5.4 %collective-permute-start.25 = (bf16[32,512]{1,0:T(8,128)(2,1)S(1)}, bf16[32,512]{1,0:T(8,128)(2,1)S(1)}, u32[]{:S(2)}, u32[]{:S(2)}) collective-permute-start(bf16[32,512]{1,0:T(8,128)(2,1)S(1)} %get-tuple-element.91), channel_id=1, source_target_pairs={{0,128},{16,144},{32,160},{48,176},{64,192},{80,208},{96,224},{112... | collective-permute-start | bytes 98312 | tf_op jit(solution)/shard_map/ppermute | solution.py:46
  76.8 5.1 %collective-permute-start.26 = (bf16[32,512]{1,0:T(8,128)(2,1)S(1)}, bf16[32,512]{1,0:T(8,128)(2,1)S(1)}, u32[]{:S(2)}, u32[]{:S(2)}) collective-permute-start(bf16[32,512]{1,0:T(8,128)(2,1)S(1)} %get-tuple-element.92), channel_id=1, source_target_pairs={{0,192},{16,208},{32,224},{48,240},{64,0},{80,16},{96,32},{112,48}... | collective-permute-start | bytes 98312 | tf_op jit(solution)/shard_map/ppermute | solution.py:46
  82.0 6.2 %collective-permute-start.27 = (bf16[128,128]{1,0:T(8,128)(2,1)S(1)}, bf16[128,128]{1,0:T(8,128)(2,1)S(1)}, u32[]{:S(2)}, u32[]{:S(2)}) collective-permute-start(bf16[128,128]{1,0:T(8,128)(2,1)S(1)} %get-tuple-element.94), channel_id=1, source_target_pairs={{0,16},{16,32},{32,48},{48,0},{64,80},{80,96},{96,112},{112,64},{1... | collective-permute-start | bytes 98312 | tf_op jit(solution)/shard_map/ppermute | solution.py:46
  83.3 4.9 %collective-permute-start.28 = (bf16[128,128]{1,0:T(8,128)(2,1)S(1)}, bf16[128,128]{1,0:T(8,128)(2,1)S(1)}, u32[]{:S(2)}, u32[]{:S(2)}) collective-permute-start(bf16[128,128]{1,0:T(8,128)(2,1)S(1)} %get-tuple-element.95), channel_id=1, source_target_pairs={{0,32},{16,48},{32,0},{48,16},{64,96},{80,112},{96,64},{112,80},{1... | collective-permute-start | bytes 98312 | tf_op jit(solution)/shard_map/ppermute | solution.py:46
  85.3 4.4 %collective-permute-start.29 = (bf16[128,128]{1,0:T(8,128)(2,1)S(1)}, bf16[128,128]{1,0:T(8,128)(2,1)S(1)}, u32[]{:S(2)}, u32[]{:S(2)}) collective-permute-start(bf16[128,128]{1,0:T(8,128)(2,1)S(1)} %get-tuple-element.96), channel_id=1, source_target_pairs={{0,48},{16,0},{32,16},{48,32},{64,112},{80,64},{96,80},{112,96},{1... | collective-permute-start | bytes 98312 | tf_op jit(solution)/shard_map/ppermute | solution.py:46
  89.8 14.0 %copy-start.2 = (bf16[2048,384]{1,0:T(8,128)(2,1)S(1)}, bf16[2048,384]{1,0:T(8,128)(2,1)}, u32[]{:S(2)}) copy-start(bf16[2048,384]{1,0:T(8,128)(2,1)} %dec.1) | copy-start | bytes 4718596
  90.3 1.5 %collective-permute-start.30 = (f32[128,384]{1,0:T(8,128)S(1)}, f32[128,384]{1,0:T(8,128)S(1)}, u32[]{:S(2)}, u32[]{:S(2)}) collective-permute-start(f32[128,384]{1,0:T(8,128)S(1)} %get-tuple-element.100), channel_id=1, source_target_pairs={{0,1},{1,0},{2,3},{3,2},{4,5},{5,4},{6,7},{7,6},{8,9},{9,8},{10,11... | collective-permute-start | bytes 589832 | tf_op jit(solution)/shard_map/ppermute | solution.py:30
  91.9 5.4 %collective-permute-start.33 = (f32[32,384]{1,0:T(8,128)S(1)}, f32[32,384]{1,0:T(8,128)S(1)}, u32[]{:S(2)}, u32[]{:S(2)}) collective-permute-start(f32[32,384]{1,0:T(8,128)S(1)} %get-tuple-element.102), channel_id=1, source_target_pairs={{0,6},{1,7},{2,0},{3,1},{4,2},{5,3},{6,4},{7,5},{8,14},{9,15},{10,... | collective-permute-start | bytes 147464 | tf_op jit(solution)/shard_map/ppermute | solution.py:30
  92.3 4.9 %collective-permute-start.32 = (f32[32,384]{1,0:T(8,128)S(1)}, f32[32,384]{1,0:T(8,128)S(1)}, u32[]{:S(2)}, u32[]{:S(2)}) collective-permute-start(f32[32,384]{1,0:T(8,128)S(1)} %get-tuple-element.103), channel_id=1, source_target_pairs={{0,2},{1,3},{2,4},{3,5},{4,6},{5,7},{6,0},{7,1},{8,10},{9,11},{10,... | collective-permute-start | bytes 147464 | tf_op jit(solution)/shard_map/ppermute | solution.py:30
  95.2 5.6 %collective-permute-start.31 = (f32[32,384]{1,0:T(8,128)S(1)}, f32[32,384]{1,0:T(8,128)S(1)}, u32[]{:S(2)}, u32[]{:S(2)}) collective-permute-start(f32[32,384]{1,0:T(8,128)S(1)} %get-tuple-element.104), channel_id=1, source_target_pairs={{0,4},{1,5},{2,6},{3,7},{4,0},{5,1},{6,2},{7,3},{8,12},{9,13},{10,... | collective-permute-start | bytes 147464 | tf_op jit(solution)/shard_map/ppermute | solution.py:30
  100.8 7.8 %collective-permute-start.34 = (f32[16,384]{1,0:T(8,128)S(1)}, f32[16,384]{1,0:T(8,128)S(1)}, u32[]{:S(2)}, u32[]{:S(2)}) collective-permute-start(f32[16,384]{1,0:T(8,128)S(1)} %slice_add_fusion.4), channel_id=1, source_target_pairs={{0,8},{1,9},{2,10},{3,11},{4,12},{5,13},{6,14},{7,15},{8,0},{9,1},... | collective-permute-start | bytes 73736 | tf_op jit(solution)/shard_map/ppermute | solution.py:30
